TPU v7x, 256 devices: a whole 4x4x8 slice. The times are simulated.
256 devices in a mesh: dp: 8 (over z), graph: 32 (over x, y, core).
Axes of the slice: x: 4, y: 4, z: 8, core: 2. Of those that a mesh axis runs over, the one named last changes fastest.
Arguments:
- node_feats: bfloat16 [8, 224, 49, 256], P('dp', 'graph'), may hold values from -0.125 to 0.125
- node_grads: bfloat16 [8, 224, 49, 256], P('dp', 'graph'), may hold values from -1.75 to 1.75
- node_row: int32 [8, 224], P('dp'), may hold values from 0 to 223, as said below
- edge_src: int32 [8, 16384], P('dp', 'graph'), may hold values from 0 to 223, as said below
- edge_tgt: int32 [8, 16384], P('dp', 'graph'), may hold values from 0 to 223, as said below
- edge_rot: int32 [8, 16384], P('dp', 'graph'), may hold values from 0 to 2047
- edge_len: float32 [8, 16384], P('dp', 'graph'), may hold values from 0.5 to 11.5
- edge_count: int32 [8, 32], P('dp', 'graph'), may hold values from 64 to 512, as said below
- rotations: bfloat16 [2048, 7, 49], replicated, as said below
- w_zero: bfloat16 [1792, 1792], replicated, may hold values from -0.125 to 0.125
- w_radial: float32 [600, 256], replicated, may hold values from -3 to 3
Outputs:
- node_grad: float32 [8, 224, 49, 256], P('dp', 'graph')
- weight_grad: float32 [1792, 1792], P('graph')
Inputs may be any that keep to these rules, and one draw needn't show every extreme that they name: Each row of node_row is a permutation: atom i of a batch graph is held at row node_row[b, i], and graph index g holds rows g * 7 to (g + 1) * 7 - 1. `edge_tgt`: for every slot of the block of graph index g, the target atom is held at one of the rows g * 7 to (g + 1) * 7 - 1. `edge_src`: among the 512 slots of the block of one index of graph, at most 24 have source atoms held by the same index of graph; in every batch graph one index of graph holds the source atoms of exactly 24 live slots of every block. The first edge_count[b, g] slots of a block are live, the others are padding with valid ids; in every batch graph one index of graph has all 512 slots live. `rotations`: row l of each rotation is zero outside the coefficients of degree l (coefficients l * l to l * l + 2 l).
All inputs are finite; a program needn't handle non-finite values.
Results may differ from a plain program's by a relative error of at most 0.0041.
Values may be sent and summed in bfloat16 or wider, within the bound.
A program may use at most 256 MiB of HBM per device.

v0:
```python
import jax
import jax.numpy as jnp
from jax import lax
from jax.sharding import PartitionSpec as P

BLOCK = 256


CUTOFF = 12.0


def radial_profile(lengths, w_radial):
    gauss_count = w_radial.shape[0]
    spacing = CUTOFF / (gauss_count - 1)
    centers = jnp.arange(gauss_count).astype(jnp.float32) * spacing
    basis = jnp.exp(-0.5 / (2.0 * spacing) ** 2 * (lengths[:, None] - centers[None, :]) ** 2)
    return jnp.dot(
        basis, w_radial, precision=lax.Precision.HIGHEST, preferred_element_type=jnp.float32
    )


def find_rows(atom_ids, row_table):
    matches = atom_ids[:, None] == jnp.arange(row_table.shape[0], dtype=jnp.int32)[None, :]
    return jnp.sum(jnp.where(matches, row_table[None, :], 0), axis=1)


def forward_rows(turning, source, radial):
    rotated = jnp.einsum("bij,bjc->bic", turning, source, preferred_element_type=jnp.float32)
    return (rotated * radial[:, None, :]).astype(jnp.bfloat16)


def backward_terms(edge_in, target, turning, radial, w_zero):
    edge_grad = jnp.einsum(
        "bij,bjc->bic", turning, target, preferred_element_type=jnp.float32
    ).astype(jnp.bfloat16)
    edge_rows = edge_in.shape[0]
    flat_in = edge_in.reshape(edge_rows, -1)
    flat_grad = edge_grad.reshape(edge_rows, -1)
    weight_term = lax.dot_general(
        flat_in, flat_grad, (((0,), (0,)), ((), ())), preferred_element_type=jnp.float32
    )
    hidden = lax.dot_general(
        flat_grad, w_zero, (((1,), (1,)), ((), ())), preferred_element_type=jnp.float32
    )
    returned = (hidden.reshape(edge_in.shape) * radial[:, None, :]).astype(jnp.bfloat16)
    return (weight_term, returned)


def spread_back(turning, returned):
    return jnp.einsum("bij,bic->bjc", turning, returned, preferred_element_type=jnp.float32)


def per_device(
    node_feats,
    node_grads,
    node_row,
    edge_src,
    edge_tgt,
    edge_rot,
    edge_len,
    edge_count,
    rotations,
    w_zero,
    w_radial,
):
    node_dev = node_feats.shape[1]
    own_index = lax.axis_index("graph")
    row_table = node_row[0]
    grad_table = node_grads[0]
    source_ids = edge_src[0]
    target_rows = find_rows(edge_tgt[0], row_table) - own_index * node_dev
    turn_ids = edge_rot[0]
    lengths = edge_len[0]
    live_count = edge_count[0, 0]
    source_rows = find_rows(source_ids, row_table)
    square = w_zero.shape[0]
    blocks = (live_count + BLOCK - 1) // BLOCK
    sources_all = lax.all_gather(node_feats, "graph", axis=1, tiled=True)[0]

    def advance(step_index, carry):
        weight_acc, node_acc = carry
        first = step_index * BLOCK
        here_source = lax.dynamic_slice_in_dim(source_rows, first, BLOCK)
        here_target = lax.dynamic_slice_in_dim(target_rows, first, BLOCK)
        here_turn = lax.dynamic_slice_in_dim(turn_ids, first, BLOCK)
        here_length = lax.dynamic_slice_in_dim(lengths, first, BLOCK)
        alive_mask = (first + jnp.arange(BLOCK, dtype=jnp.int32) < live_count).astype(jnp.float32)
        radial = radial_profile(here_length, w_radial) * alive_mask[:, None]
        turning = rotations[here_turn]
        edge_in = forward_rows(turning, sources_all[here_source], radial)
        weight_term, returned = backward_terms(
            edge_in, grad_table[here_target], turning, radial, w_zero
        )
        return (
            weight_acc + weight_term,
            node_acc.at[here_source].add(spread_back(turning, returned)),
        )

    start_state = (
        jnp.zeros((square, square), jnp.float32),
        jnp.zeros(sources_all.shape, jnp.float32),
    )
    weight_acc, node_acc = lax.fori_loop(0, blocks, advance, start_state)
    node_part = lax.psum_scatter(node_acc[None], "graph", scatter_dimension=1, tiled=True)
    rows_part = lax.psum_scatter(weight_acc, "graph", scatter_dimension=0, tiled=True)
    weight_grad = lax.psum(rows_part, "dp")
    return (node_part, weight_grad)


def solution(mesh):
    placed = (
        P("dp", "graph", None, None),
        P("dp", "graph", None, None),
        P("dp", None),
        P("dp", "graph"),
        P("dp", "graph"),
        P("dp", "graph"),
        P("dp", "graph"),
        P("dp", "graph"),
        P(),
        P(),
        P(),
    )
    return jax.shard_map(
        per_device,
        mesh=mesh,
        in_specs=placed,
        out_specs=(P("dp", "graph", None, None), P("graph", None)),
        check_vma=False,
    )
```

profile of v0, /device:TPU:1, one launch (start us, length us, event | category | flops | bytes accessed | tf_op | source)
XLA Modules:
  0.0 612.6 jit_solution(6712216942642518904)
XLA Ops:
  7.2 0.0 all-gather.2.cloned.1.call-start
  7.2 0.7 all-gather.2.cloned.1.call-update
  7.9 0.0 reduce-scatter.2.cloned.1.call-start
  8.6 5.6 copy.34
  14.2 0.9 select_reduce_fusion
  15.1 54.1 %all-gather.2.cloned.1.call-done = bf16[1,224,49,256]{3,2,0,1:T(8,128)(2,1)} async-done(((bf16[1,7,49,256]{3,2,0,1:T(8,128)(2,1)}), bf16[1,224,49,256]{3,2,0,1:T(8,128)(2,1)}) %all-gather.2.cloned.1.call-update) | async-done | bytes 5619728 | tf_op jit(solution)/shard_map/all_gather | solution.py:78
  69.2 5.5 broadcast_in_dim.44
  74.8 0.0 copy-start
  74.8 0.0 copy-start.2
  74.8 0.0 copy-start.3
  74.8 0.0 copy-start.4
  74.8 5.4 broadcast_in_dim.45
  80.2 0.0 copy-done
  80.2 0.0 copy-done.2
  80.2 0.0 copy-done.3
  80.2 0.0 copy-done.4
  80.2 100.2 %while.12 = (s32[]{:T(128)}, f32[1792,1792]{1,0:T(8,128)}, f32[224,49,256]{2,1,0:T(8,128)}, s32[]{:T(128)}, s32[512]{0:T(512)S(1)}, /*index=5*/bf16[2048,7,49]{2...) while((s32[]{:T(128)}, f32[1792,1792]{1,0:T(8,128)}, ...), condition=%wide.region_4.5_spmd, body=%wide.region_2.4_spmd.sunk | while | flops 3904316672 | bytes 142397968 | solution.py:103
  80.4 0.1 compare_select_fusion.5
  80.5 3.0 gather_fusion
  83.5 0.1 compare_select_fusion.6
  83.6 6.8 %gather_fusion.1 = bf16[256,49,256]{2,1,0:T(8,128)(2,1)} fusion(bf16[224,49,256]{2,1,0:T(8,128)(2,1)} %get-tuple-element.287, s32[1024]{0:T(1024)S(1)} %pad_clamp_fusion.7), kind=kCustom, calls=%fused_computation.1.clone.1 | custom fusion | bytes 12846080 | tf_op jit(solution)/shard_map/while/body/gather | solution.py:90
  90.4 0.1 dynamic_slice.20
  90.5 0.6 compare_convert_fusion.2
  91.1 0.9 convolution_multiply_fusion.2
  92.1 4.4 multiply_convert_fusion.2
  96.5 0.8 copy.49
  97.3 4.0 gather_fusion.2
  101.3 4.4 convolution_convert_fusion.2
  105.7 1.6 copy.50
  107.3 0.0 copy-start.1
  107.3 11.9 %convolution_add_fusion.2 = f32[1792,1792]{1,0:T(8,128)} fusion(f32[1792,1792]{1,0:T(8,128)} %get-tuple-element.263, bf16[256,1792]{0,1:T(8,128)(2,1)S(1)} %bitcast.58, bf16[256,1792]{0,1:T(8,128)(2,1)} %bitcast.59), kind=kOutput, calls=%fused_computation.4.clone.1 | convolution fusion | flops 1647378432 | bytes 27525120 | tf_op jit(solution)/shard_map/while/body/dot_general | solution.py:39
  119.1 0.0 copy-done.1
  119.1 4.7 fusion.49
  123.9 7.3 %fusion.50 = f32[256,49,256]{2,1,0:T(8,128)} fusion(bf16[256,7,49]{2,1,0:T(8,128)(2,1)S(1)} %gather_fusion, f32[256,7,256]{2,0,1:T(8,128)S(1)} %fusion.49, f32[256,256]{1,0:T(8,128)S(1)} %convolution_multiply_fusion.2), kind=kOutput, calls=%fused_computation.10.clone.1 | convolution fusion | flops 45875200 | bytes 15117824 | tf_op jit(solution)/shard_map/while/body/bij,bic->bjc/dot_general | solution.py:50
  131.2 0.0 copy-start.5
  131.2 49.2 %scatter_fusion = f32[224,49,256]{2,1,0:T(8,128)} fusion(f32[224,49,256]{2,1,0:T(8,128)} %get-tuple-element.264, s32[256]{0:T(256)S(1)} %get-tuple-element.242, f32[256,49,256]{2,1,0:T(8,128)} %fusion.50), kind=kCustom, calls=%fused_computation.3.clone.1 | custom fusion | flops 3211264 | bytes 38536192 | tf_op jit(solution)/shard_map/while/body/scatter-add | solution.py:96
  180.4 0.0 copy-done.5
  180.4 0.0 reduce-scatter.2.cloned.1.call-update
  180.5 0.0 all-reduce.6.cloned.1.call-start
  180.5 14.6 %copy.36 = f32[1,224,49,256]{3,0,2,1:T(1,128)} copy(f32[1,224,49,256]{3,2,1,0:T(8,128)} %bitcast.56) | data formatting | bytes 22478848 | tf_op jit(solution)/shard_map/broadcast_in_dim | solution.py:104
  195.1 0.0 copy-start.6
  195.1 0.0 all-reduce.6.cloned.1.call-update
  195.1 0.0 all-reduce.4.cloned.1.call-start
  195.2 196.0 %reduce-scatter.2.cloned.1.call-done = f32[56,1792]{1,0:T(8,128)} async-done(((f32[1792,1792]{1,0:T(8,128)}), f32[56,1792]{1,0:T(8,128)}) %reduce-scatter.2.cloned.1.call-update) | async-done | bytes 401424 | tf_op jit(solution)/shard_map/reduce_scatter | solution.py:105
  391.2 0.0 all-reduce.4.cloned.1.call-update
  391.2 0.0 copy-done.6
  391.2 0.6 dynamic-slice
  392.5 141.1 %all-reduce.6.cloned.1.call-done = f32[1,224,49,256]{3,0,2,1:T(1,128)} async-done(((f32[1,224,49,256]{3,0,2,1:T(1,128)}), f32[1,224,49,256]{3,0,2,1:T(1,128)}) %all-reduce.6.cloned.1.call-update) | async-done | bytes 11239440
  533.6 2.0 constant_dynamic-slice_fusion
  535.6 68.8 %all-reduce.4.cloned.1.call-done = f32[56,1792]{1,0:T(8,128)} async-done(((f32[56,1792]{1,0:T(8,128)}), f32[56,1792]{1,0:T(8,128)}) %all-reduce.4.cloned.1.call-update) | async-done | bytes 401424 | tf_op jit(solution)/shard_map/psum | solution.py:106
  604.3 1.8 copy.64
  (5 shorter events, 0.0 us)
Async XLA Ops:
  7.2 62.1 %all-gather.2.cloned.1.call-start = ((), (), s32[]{:S(2)}) async-start(), calls=%async_computation.1 | async-start | bytes 6623232 | tf_op jit(solution)/shard_map/all_gather | solution.py:78
  7.9 383.3 %reduce-scatter.2.cloned.1.call-start = ((), (), s32[]{:S(2)}) async-start(), calls=%async_computation.2 | async-start | bytes 13246464 | tf_op jit(solution)/shard_map/reduce_scatter | solution.py:105
  74.8 5.4 copy-start
  74.8 5.4 copy-start.2
  74.8 5.4 copy-start.3
  74.8 5.4 copy-start.4
  107.3 11.9 %copy-start.1 = (bf16[256,7,256]{0,2,1:T(8,128)(2,1)S(1)}, bf16[256,7,256]{0,2,1:T(8,128)(2,1)}, u32[]{:S(2)}) copy-start(bf16[256,7,256]{0,2,1:T(8,128)(2,1)} %copy.50) | copy-start | bytes 2752516 | tf_op jit(solution)/shard_map/while
  131.2 49.3 %copy-start.5 = (f32[600,256]{1,0:T(8,128)S(1)}, f32[600,256]{1,0:T(8,128)}, u32[]{:S(2)}) copy-start(f32[600,256]{1,0:T(8,128)} %get-tuple-element.334) | copy-start | bytes 1843204 | tf_op jit(solution)/shard_map/while
  180.5 353.1 %all-reduce.6.cloned.1.call-start = ((), (), s32[]{:S(2)}) async-start(), calls=%async_computation.4 | async-start | bytes 22478848
  195.1 196.1 %copy-start.6 = (u32[256]{0:T(256)S(1)}, u32[256]{0:T(256)}, u32[]{:S(2)}) copy-start(u32[256]{0:T(256)} %constant.58) | copy-start | bytes 3076
  195.1 409.2 %all-reduce.4.cloned.1.call-start = ((), (), s32[]{:S(2)}) async-start(), calls=%async_computation.3 | async-start | bytes 802816 | tf_op jit(solution)/shard_map/psum | solution.py:106
Sparse Core Ops, SparseCore 0:
  10.6 58.5 all-gather.1
  180.6 210.5 reduce-scatter.1
  394.7 138.8 all-reduce.5
  535.8 68.4 all-reduce.3
where the time goes:
time: 618 us; the launch traced here: 613 us
  waiting for transfers between devices  461 us (75%)
  local copies, waits for them, and re-layouts  51.7 us (8%)
  other arithmetic  51 us (8%)
  matrix products  33.7 us (5%)
  between operations  15.1 us (2%)
    reduce_scatter x1, waiting for transfers between devices, per_device(): lax.psum_scatter(weight_acc, 'graph', scatter_dimension=0, tiled=True)  196 us
    unnamed x5, waiting for transfers between devices  142 us
    psum x1, waiting for transfers between devices, per_device(): weight_grad = lax.psum(rows_part, 'dp')  68.8 us
    all_gather x1, waiting for transfers between devices, per_device(): sources_all = lax.all_gather(node_feats, 'graph', axis=1, tiled=True)[0]  54.1 us
    scatter-add x1, other arithmetic, advance(): node_acc.at[here_source].add(spread_back(turning, returned))  49.2 us
    broadcast_in_dim x1, local copies, waits for them, and re-layouts, per_device(): node_acc[None]  14.6 us
  transfers between devices with their start and end apart: 4, of which 4 were waited for; matrix products, arithmetic and copies ran while one was open for 4% of the time, Pallas kernels for 0%

commit v1 on v0

v1 whole, which is shorter than its diff:
```python
import functools

import jax
import jax.numpy as jnp
from jax import lax
from jax.experimental import pallas as pl
from jax.experimental.pallas import tpu as pltpu
from jax.sharding import PartitionSpec as P

CUTOFF = 12.0
CAP = 24
DEG = 7
COEF = 49
ROWS = 7
CH = 256
WIDTH = DEG * CH
META = 128
WIDE = WIDTH + META
SPAN = 64 * ROWS
F32, BF16, I32 = jnp.float32, jnp.bfloat16, jnp.int32
MESH = pl.DeviceIdType.MESH
VMEM_LIMIT = 60 * 1024 * 1024


def iota(shape, dim):
    return lax.broadcasted_iota(I32, shape, dim)


def onehot(mask):
    return jnp.where(mask, 1.0, 0.0).astype(BF16)


def dot(a, b, dims=((1,), (0,))):
    return lax.dot_general(a, b, (dims, ((), ())), preferred_element_type=F32)


def spread_matrix():
    j, lane = iota((META, SPAN), 0), iota((META, SPAN), 1)
    return onehot((lane & 63 == j) & (j < COEF))


def selector(meta, column):
    wide = dot(meta.astype(BF16), spread_matrix())
    atom = meta[:, column : column + 1].astype(I32)
    return jnp.where(iota(wide.shape, 1) >> 6 == atom, wide, 0.0).astype(BF16)


def in_degree(position, degree):
    return (position >= degree * degree) & (position < (degree + 1) * (degree + 1))


def pack_nodes(nodes_ref, packed_ref):
    packed_ref[...] = jnp.zeros(packed_ref.shape, F32)
    for q in range(ROWS):
        packed_ref[q * 64 : q * 64 + COEF, :] = nodes_ref[q].astype(F32)


def send_rows_kernel(
    holders, count_ref, table_ref, src_ref, tgt_ref, rot_ref, len_ref, turns_ref, grads_ref,
    out_ref, turn_ref, rows_ref, packed_ref,
):
    own = lax.axis_index("graph")
    slots = src_ref.shape[1]
    atoms = table_ref.shape[1]
    rows = holders * CAP
    live = iota((1, slots), 1) < count_ref[0, 0]
    table = jnp.broadcast_to(table_ref[...].astype(F32), (8, atoms)).astype(BF16)

    def rows_of(ids):
        return dot(table, onehot(iota((atoms, slots), 0) == ids))[0:1].astype(I32)

    src = rows_of(src_ref[...])
    tgt = rows_of(tgt_ref[...])
    holder = (src * 9363) >> 16
    held = onehot((iota((holders, slots), 0) == holder) & live)
    before = onehot(iota((slots, slots), 0) < iota((slots, slots), 1))
    rank = jnp.sum(held.astype(F32) * dot(held, before), axis=0, keepdims=True)
    place = jnp.where(live, holder * CAP + rank.astype(I32), -1)
    chosen = onehot(iota((rows, slots), 0) == place)

    total = turns_ref[0].astype(F32)
    for degree in range(1, DEG):
        total += turns_ref[degree].astype(F32)
    turn_ref[...] = total.astype(BF16)
    step = 512
    turned = jnp.zeros((COEF, slots), F32)
    for first in range(0, turns_ref.shape[2], step):
        turned += dot(
            turn_ref[:, first : first + step],
            onehot(iota((step, slots), 0) + first == rot_ref[...]),
        )
    length = len_ref[...]
    high = length.astype(BF16).astype(F32)
    middle = (length - high).astype(BF16).astype(F32)
    rows_ref[...] = jnp.zeros(rows_ref.shape, F32)
    rows_ref[0:COEF, :] = turned
    rows_ref[49:50, :] = (src - holder * ROWS).astype(F32)
    rows_ref[50:51, :] = (tgt - own * ROWS).astype(F32)
    rows_ref[51:52, :] = jnp.ones((1, slots), F32)
    rows_ref[52:53, :] = high
    rows_ref[53:54, :] = middle
    rows_ref[54:55, :] = length - high - middle
    meta = dot(chosen, rows_ref[...].astype(BF16), ((1,), (1,)))

    pack_nodes(grads_ref, packed_ref)
    pick = selector(meta, 50)
    position = iota((SPAN, CH), 0) & 63
    for degree in range(DEG):
        part = jnp.where(in_degree(position, degree), packed_ref[...], 0.0).astype(BF16)
        grad = dot(pick, part)
        out_ref[:, :, degree * CH : (degree + 1) * CH] = grad.reshape(holders, CAP, CH).astype(BF16)
    out_ref[:, :, WIDTH:] = meta.reshape(holders, CAP, META).astype(BF16)


def exchange_kernel(n, x_ref, y_ref, keep_sem, send_sem, recv_sem):
    me = lax.axis_index("graph")
    barrier = pltpu.get_barrier_semaphore()

    def greet(k, _):
        pl.semaphore_signal(barrier, inc=1, device_id={"graph": lax.rem(me + k, n)}, device_id_type=MESH)
        return 0

    lax.fori_loop(1, n, greet, 0)
    keep = pltpu.make_async_copy(x_ref.at[me], y_ref.at[me], keep_sem)
    keep.start()
    pl.semaphore_wait(barrier, n - 1)

    def copy(k):
        peer = lax.rem(me + k, n)
        return pltpu.make_async_remote_copy(
            src_ref=x_ref.at[peer],
            dst_ref=y_ref.at[me],
            send_sem=send_sem.at[k],
            recv_sem=recv_sem.at[k],
            device_id={"graph": peer},
            device_id_type=MESH,
        )

    def begin(k, _):
        copy(k).start()
        return 0

    def landed(k, _):
        source = lax.rem(me - k + n, n)
        pltpu.make_async_remote_copy(
            src_ref=x_ref.at[source],
            dst_ref=y_ref.at[source],
            send_sem=send_sem.at[k],
            recv_sem=recv_sem.at[k],
            device_id={"graph": source},
            device_id_type=MESH,
        ).wait_recv()
        copy(k).wait_send()
        return 0

    lax.fori_loop(1, n, begin, 0)
    keep.wait()
    lax.fori_loop(1, n, landed, 0)


def edge_kernel(
    x_ref, feats_ref, w_ref, radial_ref, own_ref, other_ref, node_ref,
    packed_ref, grad_ref, in_ref, pick_ref, scale_ref, acc_ref,
):
    core = lax.rem(lax.axis_index("graph"), 2)
    rows = grad_ref.shape[0]
    half = WIDTH // 2
    for degree in range(DEG):
        cols = slice(degree * CH, (degree + 1) * CH)
        grad_ref[:, cols] = x_ref[:, :, cols].astype(F32).reshape(rows, CH).astype(BF16)
    meta = x_ref[:, :, WIDTH:].astype(F32).reshape(rows, META)
    lane = iota((rows, META), 1)
    length = jnp.sum(jnp.where((lane >= 52) & (lane < 55), meta, 0.0), axis=1, keepdims=True)
    live = meta[:, 51:52]
    gauss = radial_ref.shape[0]
    spacing = CUTOFF / (gauss - 1)
    centers = iota((1, gauss), 1).astype(F32) * spacing
    basis = jnp.exp((-0.5 / (2.0 * spacing) ** 2) * (length - centers) ** 2)
    scale_ref[...] = live * lax.dot_general(
        basis, radial_ref[...], (((1,), (0,)), ((), ())),
        precision=lax.Precision.HIGHEST, preferred_element_type=F32,
    )
    pick = selector(meta, 49)
    pick_ref[...] = pick.astype(F32).T.astype(BF16)
    pack_nodes(feats_ref, packed_ref)
    acc_ref[...] = jnp.zeros(acc_ref.shape, F32)
    position = iota((SPAN, CH), 0) & 63

    for degree in range(DEG):
        part = jnp.where(in_degree(position, degree), packed_ref[...], 0.0).astype(BF16)
        in_ref[:, degree * CH : (degree + 1) * CH] = (dot(pick, part) * scale_ref[...]).astype(BF16)

    def weights(degree, _):
        at = pl.ds(pl.multiple_of(degree * CH, CH), CH)
        turned = in_ref[:, at]
        mine = grad_ref[:, pl.ds(pl.multiple_of(core * half, 128), half)]
        own_ref[at, :] = dot(turned, mine, ((0,), (0,)))
        theirs = grad_ref[:, pl.ds(pl.multiple_of((1 - core) * half, 128), half)]
        other_ref[at, :] = dot(turned, theirs, ((0,), (0,))).astype(BF16)
        return 0

    lax.fori_loop(0, DEG, weights, 0)

    def backward(degree, _):
        at = pl.ds(pl.multiple_of(degree * CH, CH), CH)
        hidden = dot(grad_ref[...], w_ref[at, :], ((1,), (1,)))
        back = (hidden * scale_ref[...]).astype(BF16)
        term = dot(pick_ref[...], back)
        acc_ref[...] += jnp.where(in_degree(position, degree), term, 0.0)
        return 0

    lax.fori_loop(0, DEG, backward, 0)
    for q in range(ROWS):
        node_ref[q] = acc_ref[q * 64 : q * 64 + COEF, :]


def reduce_kernel(
    depth, own_ref, other_ref, out_ref,
    pair_ref, send1, recv1, acc, send2, recv2, total, send3, recv3, mine, recv4, whole, swap, both,
    ps, pr, s1, r1, s2, r2, s3, r3, s4, r4, s5, r5,
):
    me, layer = lax.axis_index("graph"), lax.axis_index("dp")
    core, place = lax.rem(me, 2), me // 2
    x, y = place // 4, lax.rem(place, 4)
    first = (1 - core) * x + core * y
    second = (1 - core) * y + core * x

    def chip(kind, a, b):
        return (1 - kind) * (a * 4 + b) + kind * (b * 4 + a)

    def along(k, m):
        a, b = lax.rem(first + k, 4), lax.rem(second + m, 4)
        return {"graph": chip(core, a, b) * 2 + core}

    partner = {"graph": place * 2 + 1 - core}

    def above(k):
        return {"dp": lax.rem(layer + k, depth)}

    barrier = pltpu.get_barrier_semaphore()
    peers = [partner] + [along(k, 0) for k in (1, 2, 3)] + [along(0, k) for k in (1, 2, 3)]
    peers += [above(k) for k in range(1, depth)]
    for peer in peers:
        pl.semaphore_signal(barrier, inc=1, device_id=peer, device_id_type=MESH)
    pl.semaphore_wait(barrier, len(peers))

    def remote(src, dst, ss, rs, peer):
        return pltpu.make_async_remote_copy(
            src_ref=src, dst_ref=dst, send_sem=ss, recv_sem=rs, device_id=peer, device_id_type=MESH
        )

    def pair(n):
        k, i = lax.rem(n // 4 + 1, 4), lax.rem(n, 4)
        block = chip(1 - core, lax.rem(second + k, 4), i)
        return remote(other_ref.at[block], pair_ref.at[n], ps.at[n], pr.at[n], partner)

    def pair_start(n, _):
        pair(n).start()
        return 0

    lax.fori_loop(0, 16, pair_start, 0)

    def out1(k, i):
        return remote(send1.at[k - 1, i], recv1.at[k - 1, i], s1.at[k - 1, i], r1.at[k - 1, i], along(k, 0))

    for k in (1, 2, 3):

        def step1(i, _, k=k):
            n = (k - 1) * 4 + i
            pair(n).wait_recv()
            block = chip(core, lax.rem(first + k, 4), i)
            send1[k - 1, i] = (own_ref[block] + pair_ref[n].astype(F32)).astype(BF16)
            out1(k, i).start()
            return 0

        lax.fori_loop(0, 4, step1, 0)

    def keep1(i, _):
        pair(12 + i).wait_recv()
        acc[i] = own_ref[chip(core, first, i)] + pair_ref[12 + i].astype(F32)
        return 0

    lax.fori_loop(0, 4, keep1, 0)

    def gathered(i):
        for k in (1, 2, 3):
            out1(k, i).wait_recv()
        got = acc[i]
        for k in (0, 1, 2):
            got += recv1[k, i].astype(F32)
        return got

    def out2(m):
        return remote(send2.at[m - 1], recv2.at[m - 1], s2.at[m - 1], r2.at[m - 1], along(0, m))

    for m in (1, 2, 3):
        send2[m - 1] = gathered(lax.rem(second + m, 4)).astype(BF16)
        out2(m).start()
    kept = gathered(second)
    for m in (1, 2, 3):
        out2(m).wait_recv()
        kept += recv2[m - 1].astype(F32)
    rows = kept.shape[0]
    total[0:rows, :] = kept
    total[rows:, :] = jnp.zeros((total.shape[0] - rows, kept.shape[1]), F32)
    send3[...] = total[...].astype(BF16).reshape(send3.shape)

    def out3(k):
        return remote(
            send3.at[lax.rem(layer + k, depth)], recv3.at[k - 1], s3.at[k - 1], r3.at[k - 1], above(k)
        )

    for k in range(1, depth):
        out3(k).start()
    part = total[pl.ds(pl.multiple_of(layer * 16, 16), 16), :]
    for k in range(1, depth):
        out3(k).wait_recv()
        part += recv3[k - 1].astype(F32)
    mine[...] = part.astype(BF16)

    def out4(k):
        return remote(mine, recv4.at[k - 1], s4.at[k - 1], r4.at[k - 1], above(k))

    for k in range(1, depth):
        out4(k).start()
    whole[layer] = mine[...]
    for k in range(1, depth):
        out4(k).wait_recv()
        whole[lax.rem(layer - k + depth, depth)] = recv4[k - 1]
    out5 = remote(whole, swap, s5, r5, partner)
    out5.start()
    half = kept.shape[1]
    row = pl.ds(pl.multiple_of(core * 56, 8), 56)
    both[...] = whole[...].astype(F32).reshape(both.shape)
    out_ref[:, pl.ds(pl.multiple_of(core * half, 128), half)] = both[row, :]
    out5.wait_recv()
    both[...] = swap[...].astype(F32).reshape(both.shape)
    out_ref[:, pl.ds(pl.multiple_of((1 - core) * half, 128), half)] = both[row, :]

    def pair_done(n, _):
        pair(n).wait_send()
        return 0

    lax.fori_loop(0, 16, pair_done, 0)
    for k in (1, 2, 3):
        for i in range(4):
            out1(k, i).wait_send()
        out2(k).wait_send()
    for k in range(1, depth):
        out3(k).wait_send()
        out4(k).wait_send()
    out5.wait_send()


def vmem():
    return pl.BlockSpec(memory_space=pltpu.VMEM)


def per_device(
    node_feats, node_grads, node_row, edge_src, edge_tgt, edge_rot, edge_len, edge_count, rotations, w_zero, w_radial,
    holders, depth,
):
    slots = edge_src.shape[1]
    turns = rotations.transpose(1, 2, 0)
    rows = holders * CAP
    half = WIDTH // 2
    params = functools.partial(pltpu.CompilerParams, vmem_limit_bytes=VMEM_LIMIT)
    wide = jax.ShapeDtypeStruct((holders, CAP, WIDE), BF16)
    sent = pl.pallas_call(
        functools.partial(send_rows_kernel, holders),
        out_shape=wide,
        in_specs=[pl.BlockSpec(memory_space=pltpu.SMEM)] + [vmem()] * 7,
        out_specs=vmem(),
        scratch_shapes=[
            pltpu.VMEM((COEF, turns.shape[2]), BF16),
            pltpu.VMEM((META, slots), F32),
            pltpu.VMEM((SPAN, CH), F32),
        ],
        compiler_params=params(),
        name="send_rows",
    )(edge_count, node_row, edge_src, edge_tgt, edge_rot, edge_len, turns, node_grads[0])
    anywhere = pl.BlockSpec(memory_space=pl.ANY)
    dma = pltpu.SemaphoreType.DMA
    got = pl.pallas_call(
        functools.partial(exchange_kernel, holders),
        out_shape=wide,
        in_specs=[anywhere],
        out_specs=anywhere,
        scratch_shapes=[dma, dma((holders,)), dma((holders,))],
        compiler_params=pltpu.CompilerParams(collective_id=0, has_side_effects=True),
        name="exchange",
    )(sent)
    own, other, node = pl.pallas_call(
        edge_kernel,
        out_shape=(
            jax.ShapeDtypeStruct((WIDTH, half), F32),
            jax.ShapeDtypeStruct((WIDTH, half), BF16),
            jax.ShapeDtypeStruct((ROWS, COEF, CH), F32),
        ),
        in_specs=[vmem()] * 4,
        out_specs=(vmem(),) * 3,
        scratch_shapes=[
            pltpu.VMEM((SPAN, CH), F32),
            pltpu.VMEM((rows, WIDTH), BF16),
            pltpu.VMEM((rows, WIDTH), BF16),
            pltpu.VMEM((SPAN, rows), BF16),
            pltpu.VMEM((rows, CH), F32),
            pltpu.VMEM((SPAN, CH), F32),
        ],
        compiler_params=params(),
        name="edges",
    )(got, node_feats[0], w_zero, w_radial)
    chips = holders // 2
    tall = WIDTH // chips
    block = (tall, half)
    weight = pl.pallas_call(
        functools.partial(reduce_kernel, depth),
        out_shape=jax.ShapeDtypeStruct((WIDTH // holders, WIDTH), F32),
        in_specs=[vmem(), anywhere],
        out_specs=vmem(),
        scratch_shapes=[
            pltpu.VMEM((chips, *block), BF16),
            pltpu.VMEM((3, 4, *block), BF16),
            pltpu.VMEM((3, 4, *block), BF16),
            pltpu.VMEM((4, *block), F32),
            pltpu.VMEM((3, *block), BF16),
            pltpu.VMEM((3, *block), BF16),
            pltpu.VMEM((depth * 16, half), F32),
            pltpu.VMEM((depth, 16, half), BF16),
            pltpu.VMEM((depth - 1, 16, half), BF16),
            pltpu.VMEM((16, half), BF16),
            pltpu.VMEM((depth - 1, 16, half), BF16),
            pltpu.VMEM((depth, 16, half), BF16),
            pltpu.VMEM((depth, 16, half), BF16),
            pltpu.VMEM((depth * 16, half), F32),
            dma((16,)), dma((16,)),
            dma((3, 4)), dma((3, 4)),
            dma((3,)), dma((3,)),
            dma((depth - 1,)), dma((depth - 1,)),
            dma((depth - 1,)), dma((depth - 1,)),
            dma, dma,
        ],
        compiler_params=params(collective_id=1, has_side_effects=True),
        name="reduce_weights",
    )(own.reshape(chips, *block), other.reshape(chips, *block))
    return (node[None], weight)


def solution(mesh):
    graph = P("dp", "graph")
    placed = (
        P("dp", "graph", None, None), P("dp", "graph", None, None), P("dp", None),
        graph, graph, graph, graph, graph, P(), P(), P(),
    )
    return jax.shard_map(
        functools.partial(per_device, holders=mesh.shape["graph"], depth=mesh.shape["dp"]),
        mesh=mesh,
        in_specs=placed,
        out_specs=(P("dp", "graph", None, None), P("graph", None)),
        check_vma=False,
    )
```

time: 618 us -> 167 us (0.27)
  waiting for transfers between devices: 461 us -> 0 us
  Pallas kernels: 0 us -> 162 us
  other arithmetic: 51 us -> 0 us
  local copies, waits for them, and re-layouts: 51.7 us -> 3.86 us
  matrix products: 33.7 us -> 0 us
  between operations: 15.1 us -> 1.3 us
    reduce_scatter x1 -> x0, waiting for transfers between devices: 196 us -> none  [per_device(): lax.psum_scatter(weight_acc, 'graph', scatter_dimension=0, tiled=True)]
    pallas_call x0 -> x4, Pallas kernels: none -> 162 us  [the longest x1 66.3 us: per_device(): pl.pallas_call(functools.partial(reduce_kernel, depth), out_shape=jax.Sha...]
    unnamed x5 -> x0, waiting for transfers between devices: 142 us -> none
    psum x1 -> x0, waiting for transfers between devices: 68.8 us -> none  [per_device(): weight_grad = lax.psum(rows_part, 'dp')]
    all_gather x1 -> x0, waiting for transfers between devices: 54.1 us -> none  [per_device(): sources_all = lax.all_gather(node_feats, 'graph', axis=1, tiled=True)[0]]
    scatter-add x1 -> x0, other arithmetic: 49.2 us -> none  [advance(): node_acc.at[here_source].add(spread_back(turning, returned))]
    dot_general x6 -> x0, matrix products: 33.7 us -> none  [the longest x1 11.9 us: backward_terms(): lax.dot_general(flat_in, flat_grad, (((0,), (0,)), ((), ())), preferred_e...]
    broadcast_in_dim x3 -> x0, local copies, waits for them, and re-layouts: 25.5 us -> none  [the longest x1 14.6 us: per_device(): node_acc[None]]
  transfers between devices with their start and end apart: 4 -> 0, of which waited for: 4 -> 0; matrix products, arithmetic and copies ran while one was open for 4% -> 0% of each run, Pallas kernels for 0% -> 0%
where the time goes in v1:
time: 167 us
  Pallas kernels  162 us (97%)
  local copies, waits for them, and re-layouts  3.86 us (2%)
    pallas_call x1, Pallas kernels, per_device(): pl.pallas_call(functools.partial(reduce_kernel, depth), out_shape=jax.Sha...  66.3 us
    pallas_call x1, Pallas kernels, per_device(): pl.pallas_call(functools.partial(exchange_kernel, holders), out_shape=wid...  61.1 us
    pallas_call x1, Pallas kernels, per_device(): pl.pallas_call(edge_kernel, out_shape=(jax.ShapeDtypeStruct((WIDTH, half)...  28 us
    pallas_call x1, Pallas kernels, per_device(): pl.pallas_call(functools.partial(send_rows_kernel, holders), out_shape=wi...  6.24 us
    unnamed x2, local copies, waits for them, and re-layouts  3.86 us

profile of v1, /device:TPU:1, one launch (start us, length us, event | category | flops | bytes accessed | tf_op | source)
XLA Modules:
  0.0 166.8 jit_solution(17223712250398512773)
XLA Ops:
  1.3 6.2 %send_rows.1.x_ref = bf16[32,24,1920]{2,1,0:T(8,128)(2,1)} custom-call(s32[1,1]{1,0:T(1,128)S(6)} %copy.15.count_ref, s32[1,224]{1,0:T(1,128)} %table_ref.1, s32[1,512]{1,0:T(1,128)} %src_ref.1, s32[1,512]{1,0:T(1,128)} %tgt_ref.1, s32[1,512]{1,0:T(1,128)} %rot_ref.1, f32[1,512]{1,0:T(1,128)} %len_ref.1, bf16[7,49,2048]{2,1,0:T(8,128)(2,1)} %bitcast.8, ...), custom_call_target="tpu_custom_call" | custom-call | tf_op jit(solution)/shard_map/send_rows/pallas_call | solution.py:369
  7.5 61.1 %exchange.1.x_ref = bf16[32,24,1920]{2,1,0:T(8,128)(2,1)} custom-call(bf16[32,24,1920]{2,1,0:T(8,128)(2,1)} %send_rows.1.x_ref), custom_call_target="tpu_custom_call" | custom-call | tf_op jit(solution)/shard_map/exchange/pallas_call | solution.py:384
  68.7 28.0 %edges.1 = (f32[1792,896]{1,0:T(8,128)}, bf16[1792,896]{1,0:T(8,128)(2,1)}, f32[7,49,256]{2,1,0:T(8,128)}) custom-call(bf16[32,24,1920]{2,1,0:T(8,128)(2,1)} %exchange.1.x_ref, bf16[7,49,256]{2,1,0:T(8,128)(2,1)} %bitcast.11, bf16[1792,1792]{1,0:T(8,128)(2,1)} %w_ref.1, f32[600,256]{1,0:T(8,128)} %radial_ref.1), custom_call_target="tpu_custom_call" | custom-call | tf_op jit(solution)/shard_map/edges/pallas_call | solution.py:393
  96.6 2.1 %copy.13 = f32[1,7,49,256]{3,0,2,1:T(1,128)} copy(f32[1,7,49,256]{3,2,1,0:T(8,128)} %bitcast.9) | data formatting | bytes 702464
  98.7 66.3 %reduce_weights.1 = f32[56,1792]{1,0:T(8,128)} custom-call(f32[16,112,896]{2,1,0:T(8,128)} %bitcast.6, bf16[16,112,896]{2,1,0:T(8,128)(2,1)} %bitcast.7), custom_call_target="tpu_custom_call" | custom-call | tf_op jit(solution)/shard_map/reduce_weights/pallas_call | solution.py:416
  165.1 1.8 %copy.16 = f32[56,1792]{1,0:T(8,128)} copy(f32[56,1792]{1,0:T(8,128)} %reduce_weights.1) | data formatting | bytes 802816

commit v2 on v1

v2 whole, which is shorter than its diff:
```python
import functools

import jax
import jax.numpy as jnp
from jax import lax
from jax.experimental import pallas as pl
from jax.experimental.pallas import tpu as pltpu
from jax.sharding import PartitionSpec as P

CUTOFF = 12.0
CAP = 24
DEG = 7
COEF = 49
ROWS = 7
CH = 256
WIDTH = DEG * CH
META = 128
HALF = WIDTH // 2
TALL = 112
SPAN = 64 * ROWS
F32, BF16, I32 = jnp.float32, jnp.bfloat16, jnp.int32
MESH = pl.DeviceIdType.MESH
VMEM_LIMIT = 60 * 1024 * 1024
FAR = (
    (2, 2), (2, 1), (1, 2), (2, 3), (3, 2), (2, 0), (0, 2), (1, 1),
    (3, 3), (1, 3), (3, 1), (1, 0), (0, 1), (3, 0), (0, 3),
)
STEPS = [(a, b, c) for c in (0, 1) for a, b in FAR] + [(0, 0, 1)]


def iota(shape, dim):
    return lax.broadcasted_iota(I32, shape, dim)


def onehot(mask):
    return jnp.where(mask, 1.0, 0.0).astype(BF16)


def dot(a, b, dims=((1,), (0,))):
    return lax.dot_general(a, b, (dims, ((), ())), preferred_element_type=F32)


def spread_matrix():
    j, lane = iota((META, SPAN), 0), iota((META, SPAN), 1)
    return onehot((lane & 63 == j) & (j < COEF))


def selector(meta, column):
    wide = dot(meta.astype(BF16), spread_matrix())
    atom = meta[:, column : column + 1].astype(I32)
    return jnp.where(iota(wide.shape, 1) >> 6 == atom, wide, 0.0).astype(BF16)


def in_degree(position, degree):
    return (position >= degree * degree) & (position < (degree + 1) * (degree + 1))


def pack_nodes(nodes_ref, packed_ref):
    packed_ref[...] = jnp.zeros(packed_ref.shape, F32)
    for q in range(ROWS):
        packed_ref[q * 64 : q * 64 + COEF, :] = nodes_ref[q].astype(F32)


def find_meta(holders, count_ref, table_ref, src_ref, tgt_ref, rot_ref, len_ref, turns_ref, turn_ref, rows_ref):
    own = lax.axis_index("graph")
    slots = src_ref.shape[1]
    atoms = table_ref.shape[1]
    live = iota((1, slots), 1) < count_ref[0, 0]
    table = jnp.broadcast_to(table_ref[...].astype(F32), (8, atoms)).astype(BF16)

    def rows_of(ids):
        return dot(table, onehot(iota((atoms, slots), 0) == ids))[0:1].astype(I32)

    src = rows_of(src_ref[...])
    tgt = rows_of(tgt_ref[...])
    holder = (src * 9363) >> 16
    held = onehot((iota((holders, slots), 0) == holder) & live)
    before = onehot(iota((slots, slots), 0) < iota((slots, slots), 1))
    rank = jnp.sum(held.astype(F32) * dot(held, before), axis=0, keepdims=True)
    place = jnp.where(live, holder * CAP + rank.astype(I32), -1)
    chosen = onehot(iota((holders * CAP, slots), 0) == place)

    total = turns_ref[0].astype(F32)
    for degree in range(1, DEG):
        total += turns_ref[degree].astype(F32)
    turn_ref[...] = total.astype(BF16)
    step = 512
    turned = jnp.zeros((COEF, slots), F32)
    for start in range(0, turns_ref.shape[2], step):
        turned += dot(
            turn_ref[:, start : start + step],
            onehot(iota((step, slots), 0) + start == rot_ref[...]),
        )
    length = len_ref[...]
    high = length.astype(BF16).astype(F32)
    middle = (length - high).astype(BF16).astype(F32)
    rows_ref[...] = jnp.zeros(rows_ref.shape, F32)
    rows_ref[0:COEF, :] = turned
    rows_ref[49:50, :] = (src - holder * ROWS).astype(F32)
    rows_ref[50:51, :] = (tgt - own * ROWS).astype(F32)
    rows_ref[51:52, :] = jnp.ones((1, slots), F32)
    rows_ref[52:53, :] = high
    rows_ref[53:54, :] = middle
    rows_ref[54:55, :] = length - high - middle
    return dot(chosen, rows_ref[...].astype(BF16), ((1,), (1,)))


def layer_kernel(
    holders, depth,
    count_ref, table_ref, src_ref, tgt_ref, rot_ref, len_ref, turns_ref, grads_ref, feats_ref, radial_ref, w_hbm,
    node_ref, out_ref,
    turn_ref, rows_ref, packed_ref, meta_out, meta_in, grad_out, grad_in, w_ref,
    grad_ref, in_ref, pick_ref, scale_ref, acc_ref, own_ref, other_ref,
    pair_ref, send1, recv1, part1, send2, recv2, total, send3, recv3, mine, recv4, whole, swap, both,
    ws, ms, mr, gs, gr, ps, pr, s1, r1, s2, r2, s3, r3, s4, r4, s5, r5,
):
    me, layer = lax.axis_index("graph"), lax.axis_index("dp")
    core, place = lax.rem(me, 2), me // 2
    x, y = place // 4, lax.rem(place, 4)
    rows = holders * CAP
    first = (1 - core) * x + core * y
    second = (1 - core) * y + core * x

    def chip(kind, a, b):
        return (1 - kind) * (a * 4 + b) + kind * (b * 4 + a)

    def index(a, b, c):
        return chip(core, lax.rem(first + a, 4), lax.rem(second + b, 4)) * 2 + lax.rem(core + c, 2)

    def along(a, b):
        return {"graph": index(a, b, 0)}

    partner = {"graph": index(0, 0, 1)}

    def above(k):
        return {"dp": lax.rem(layer + k, depth)}

    def remote(src, dst, ss, rs, peer):
        return pltpu.make_async_remote_copy(
            src_ref=src, dst_ref=dst, send_sem=ss, recv_sem=rs, device_id=peer, device_id_type=MESH
        )

    load_w = pltpu.make_async_copy(w_hbm, w_ref, ws)
    load_w.start()
    barrier = pltpu.get_barrier_semaphore()
    for a, b, c in STEPS:
        pl.semaphore_signal(barrier, inc=1, device_id={"graph": index(a, b, c)}, device_id_type=MESH)
    for k in range(1, depth):
        pl.semaphore_signal(barrier, inc=1, device_id=above(k), device_id_type=MESH)

    meta = find_meta(
        holders, count_ref, table_ref, src_ref, tgt_ref, rot_ref, len_ref, turns_ref, turn_ref, rows_ref
    )
    meta_out[...] = meta.reshape(holders, CAP, META).astype(BF16)
    pl.semaphore_wait(barrier, len(STEPS) + depth - 1)

    def meta_copy(k):
        peer = index(*STEPS[k - 1])
        return remote(meta_out.at[peer], meta_in.at[k], ms.at[k], mr.at[k], {"graph": peer})

    def grad_copy(k):
        peer = index(*STEPS[k - 1])
        return remote(grad_out.at[peer], grad_in.at[k], gs.at[k], gr.at[k], {"graph": peer})

    for k in range(1, holders):
        meta_copy(k).start()
    pack_nodes(grads_ref, packed_ref)
    pick = selector(meta, 50)
    position = iota((SPAN, CH), 0) & 63
    for degree in range(DEG):
        part = jnp.where(in_degree(position, degree), packed_ref[...], 0.0).astype(BF16)
        grad = dot(pick, part)
        grad_out[:, :, degree * CH : (degree + 1) * CH] = grad.reshape(holders, CAP, CH).astype(BF16)
    for k in range(1, holders):
        grad_copy(k).start()
    meta_in[0] = meta_out[me]
    grad_in[0] = grad_out[me]

    for k in range(1, holders):
        meta_copy(k).wait_recv()
    meta = meta_in[...].astype(F32).reshape(rows, META)
    lane = iota((rows, META), 1)
    length = jnp.sum(jnp.where((lane >= 52) & (lane < 55), meta, 0.0), axis=1, keepdims=True)
    live = meta[:, 51:52]
    gauss = radial_ref.shape[0]
    spacing = CUTOFF / (gauss - 1)
    centers = iota((1, gauss), 1).astype(F32) * spacing
    basis = jnp.exp((-0.5 / (2.0 * spacing) ** 2) * (length - centers) ** 2)
    scale_ref[...] = live * lax.dot_general(
        basis, radial_ref[...], (((1,), (0,)), ((), ())),
        precision=lax.Precision.HIGHEST, preferred_element_type=F32,
    )
    pick = selector(meta, 49)
    pick_ref[...] = pick.astype(F32).T.astype(BF16)
    pack_nodes(feats_ref, packed_ref)
    for degree in range(DEG):
        part = jnp.where(in_degree(position, degree), packed_ref[...], 0.0).astype(BF16)
        in_ref[:, degree * CH : (degree + 1) * CH] = (dot(pick, part) * scale_ref[...]).astype(BF16)
    acc_ref[...] = jnp.zeros(acc_ref.shape, F32)
    for k in range(1, holders):
        grad_copy(k).wait_recv()
    for degree in range(DEG):
        cols = slice(degree * CH, (degree + 1) * CH)
        grad_ref[:, cols] = grad_in[:, :, cols].astype(F32).reshape(rows, CH).astype(BF16)

    def columns(kind):
        return pl.ds(pl.multiple_of(kind * HALF, 128), HALF)

    def weights_other(degree, _):
        at = pl.ds(pl.multiple_of(degree * CH, CH), CH)
        other_ref[at, :] = dot(in_ref[:, at], grad_ref[:, columns(1 - core)], ((0,), (0,))).astype(BF16)
        return 0

    lax.fori_loop(0, DEG, weights_other, 0)

    def block_of(kind, n):
        m, k = lax.rem(n // 4 + 1, 4), lax.rem(n + 1, 4)
        a = lax.rem((1 - kind) * x + kind * y + k, 4)
        b = lax.rem((1 - kind) * y + kind * x + m, 4)
        return pl.ds(pl.multiple_of(chip(kind, a, b) * TALL, 16), TALL)

    def pair(n):
        return remote(other_ref.at[block_of(1 - core, n)], pair_ref.at[n], ps.at[n], pr.at[n], partner)

    def pair_start(n, _):
        pair(n).start()
        return 0

    lax.fori_loop(0, 16, pair_start, 0)

    def weights_own(degree, _):
        at = pl.ds(pl.multiple_of(degree * CH, CH), CH)
        own_ref[at, :] = dot(in_ref[:, at], grad_ref[:, columns(core)], ((0,), (0,)))
        return 0

    lax.fori_loop(0, DEG, weights_own, 0)

    def paired(n):
        pair(n).wait_recv()
        return own_ref[block_of(core, n), :] + pair_ref[n].astype(F32)

    def out1(i, k):
        return remote(send1.at[i, k - 1], recv1.at[i, k - 1], s1.at[i, k - 1], r1.at[i, k - 1], along(k, 0))

    def step1(i, _):
        for k in (1, 2, 3):
            send1[i, k - 1] = paired(i * 4 + k - 1).astype(BF16)
            out1(i, k).start()
        part1[i] = paired(i * 4 + 3)
        return 0

    lax.fori_loop(0, 4, step1, 0)

    load_w.wait()

    def backward(degree, _):
        at = pl.ds(pl.multiple_of(degree * CH, CH), CH)
        hidden = dot(grad_ref[...], w_ref[at, :], ((1,), (1,)))
        back = (hidden * scale_ref[...]).astype(BF16)
        term = dot(pick_ref[...], back)
        acc_ref[...] += jnp.where(in_degree(position, degree), term, 0.0)
        return 0

    lax.fori_loop(0, DEG, backward, 0)
    for q in range(ROWS):
        node_ref[q] = acc_ref[q * 64 : q * 64 + COEF, :]

    def gathered(i):
        got = part1[i]
        for k in (1, 2, 3):
            out1(i, k).wait_recv()
            got += recv1[i, k - 1].astype(F32)
        return got

    def out2(m):
        return remote(send2.at[m - 1], recv2.at[m - 1], s2.at[m - 1], r2.at[m - 1], along(0, m))

    for m in (1, 2, 3):
        send2[m - 1] = gathered(m - 1).astype(BF16)
        out2(m).start()
    kept = gathered(3)
    for m in (1, 2, 3):
        out2(m).wait_recv()
        kept += recv2[m - 1].astype(F32)
    total[0:TALL, :] = kept
    total[TALL:, :] = jnp.zeros((total.shape[0] - TALL, HALF), F32)
    send3[...] = total[...].astype(BF16).reshape(send3.shape)

    def out3(k):
        return remote(
            send3.at[lax.rem(layer + k, depth)], recv3.at[k - 1], s3.at[k - 1], r3.at[k - 1], above(k)
        )

    for k in range(1, depth):
        out3(k).start()
    part = total[pl.ds(pl.multiple_of(layer * 16, 16), 16), :]
    for k in range(1, depth):
        out3(k).wait_recv()
        part += recv3[k - 1].astype(F32)
    mine[...] = part.astype(BF16)

    def out4(k):
        return remote(mine, recv4.at[k - 1], s4.at[k - 1], r4.at[k - 1], above(k))

    for k in range(1, depth):
        out4(k).start()
    whole[layer] = mine[...]
    for k in range(1, depth):
        out4(k).wait_recv()
        whole[lax.rem(layer - k + depth, depth)] = recv4[k - 1]
    out5 = remote(whole, swap, s5, r5, partner)
    out5.start()
    row = pl.ds(pl.multiple_of(core * 56, 8), 56)
    both[...] = whole[...].astype(F32).reshape(both.shape)
    out_ref[:, columns(core)] = both[row, :]
    out5.wait_recv()
    both[...] = swap[...].astype(F32).reshape(both.shape)
    out_ref[:, columns(1 - core)] = both[row, :]

    for k in range(1, holders):
        meta_copy(k).wait_send()
        grad_copy(k).wait_send()

    def pair_done(n, _):
        pair(n).wait_send()
        return 0

    lax.fori_loop(0, 16, pair_done, 0)
    for k in (1, 2, 3):
        for i in range(4):
            out1(i, k).wait_send()
        out2(k).wait_send()
    for k in range(1, depth):
        out3(k).wait_send()
        out4(k).wait_send()
    out5.wait_send()


def per_device(
    node_feats, node_grads, node_row, edge_src, edge_tgt, edge_rot, edge_len, edge_count, rotations, w_zero, w_radial,
    holders, depth,
):
    slots = edge_src.shape[1]
    turns = rotations.transpose(1, 2, 0)
    rows = holders * CAP
    block = (TALL, HALF)
    vmem = pl.BlockSpec(memory_space=pltpu.VMEM)
    dma = pltpu.SemaphoreType.DMA
    buffer = pltpu.VMEM
    node, weight = pl.pallas_call(
        functools.partial(layer_kernel, holders, depth),
        out_shape=(
            jax.ShapeDtypeStruct((ROWS, COEF, CH), F32),
            jax.ShapeDtypeStruct((WIDTH // holders, WIDTH), F32),
        ),
        in_specs=[pl.BlockSpec(memory_space=pltpu.SMEM)] + [vmem] * 9 + [pl.BlockSpec(memory_space=pl.ANY)],
        out_specs=(vmem, vmem),
        scratch_shapes=[
            buffer((COEF, turns.shape[2]), BF16),
            buffer((META, slots), F32),
            buffer((SPAN, CH), F32),
            buffer((holders, CAP, META), BF16),
            buffer((holders, CAP, META), BF16),
            buffer((holders, CAP, WIDTH), BF16),
            buffer((holders, CAP, WIDTH), BF16),
            buffer((WIDTH, WIDTH), BF16),
            buffer((rows, WIDTH), BF16),
            buffer((rows, WIDTH), BF16),
            buffer((SPAN, rows), BF16),
            buffer((rows, CH), F32),
            buffer((SPAN, CH), F32),
            buffer((WIDTH, HALF), F32),
            buffer((WIDTH, HALF), BF16),
            buffer((16, *block), BF16),
            buffer((4, 3, *block), BF16),
            buffer((4, 3, *block), BF16),
            buffer((4, *block), F32),
            buffer((3, *block), BF16),
            buffer((3, *block), BF16),
            buffer((depth * 16, HALF), F32),
            buffer((depth, 16, HALF), BF16),
            buffer((depth - 1, 16, HALF), BF16),
            buffer((16, HALF), BF16),
            buffer((depth - 1, 16, HALF), BF16),
            buffer((depth, 16, HALF), BF16),
            buffer((depth, 16, HALF), BF16),
            buffer((depth * 16, HALF), F32),
            dma,
            dma((holders,)), dma((holders,)),
            dma((holders,)), dma((holders,)),
            dma((16,)), dma((16,)),
            dma((4, 3)), dma((4, 3)),
            dma((3,)), dma((3,)),
            dma((depth - 1,)), dma((depth - 1,)),
            dma((depth - 1,)), dma((depth - 1,)),
            dma, dma,
        ],
        compiler_params=pltpu.CompilerParams(
            collective_id=0, has_side_effects=True, vmem_limit_bytes=VMEM_LIMIT
        ),
        name="layer",
    )(
        edge_count, node_row, edge_src, edge_tgt, edge_rot, edge_len, turns,
        node_grads[0], node_feats[0], w_radial, w_zero,
    )
    return (node[None], weight)


def solution(mesh):
    graph = P("dp", "graph")
    placed = (
        P("dp", "graph", None, None), P("dp", "graph", None, None), P("dp", None),
        graph, graph, graph, graph, graph, P(), P(), P(),
    )
    return jax.shard_map(
        functools.partial(per_device, holders=mesh.shape["graph"], depth=mesh.shape["dp"]),
        mesh=mesh,
        in_specs=placed,
        out_specs=(P("dp", "graph", None, None), P("graph", None)),
        check_vma=False,
    )
```

time: 167 us -> 106 us (0.63)
  Pallas kernels: 162 us -> 101 us
    pallas_call x4 -> x1, Pallas kernels: 162 us -> 101 us  [per_device(): pl.pallas_call(functools.partial(layer_kernel, holders, depth), out_shape...]
where the time goes in v2:
time: 106 us
  Pallas kernels  101 us (95%)
  local copies, waits for them, and re-layouts  3.86 us (4%)
  between operations  1.29 us (1%)
    pallas_call x1, Pallas kernels, per_device(): pl.pallas_call(functools.partial(layer_kernel, holders, depth), out_shape...  101 us
    unnamed x2, local copies, waits for them, and re-layouts  3.86 us

profile of v2, /device:TPU:1, one launch (start us, length us, event | category | flops | bytes accessed | tf_op | source)
XLA Modules:
  0.0 105.7 jit_solution(3689384158881502526)
XLA Ops:
  1.3 100.5 %layer.1 = (f32[7,49,256]{2,1,0:T(8,128)}, f32[56,1792]{1,0:T(8,128)}) custom-call(s32[1,1]{1,0:T(1,128)S(6)} %copy.15.count_ref, s32[1,224]{1,0:T(1,128)} %table_ref.1, s32[1,512]{1,0:T(1,128)} %src_ref.1, s32[1,512]{1,0:T(1,128)} %tgt_ref.1, s32[1,512]{1,0:T(1,128)} %rot_ref.1, f32[1,512]{1,0:T(1,128)} %len_ref.1, bf16[7,49,2048]{2,1,0:T(8,128)(2,1)} %bitcast.4, ...), custom_call_target="tpu_custom_call" | custom-call | tf_op jit(solution)/shard_map/layer/pallas_call | solution.py:350
  101.8 2.1 %copy.13 = f32[1,7,49,256]{3,0,2,1:T(1,128)} copy(f32[1,7,49,256]{3,2,1,0:T(8,128)} %bitcast.5) | data formatting | bytes 702464
  103.9 1.8 %copy.16 = f32[56,1792]{1,0:T(8,128)} copy(f32[56,1792]{1,0:T(8,128)} %get-tuple-element.11) | data formatting | bytes 802816

commit v3 on v2

--- a/solution.py
+++ b/solution.py
@@ -17,6 +17,7 @@
 META = 128
 HALF = WIDTH // 2
 TALL = 112
+PARTS = ((0, 512), (512, 384))
 SPAN = 64 * ROWS
 F32, BF16, I32 = jnp.float32, jnp.bfloat16, jnp.int32
 MESH = pl.DeviceIdType.MESH
@@ -25,6 +26,7 @@
     (2, 2), (2, 1), (1, 2), (2, 3), (3, 2), (2, 0), (0, 2), (1, 1),
     (3, 3), (1, 3), (3, 1), (1, 0), (0, 1), (3, 0), (0, 3),
 )
+GROUPS = ((0, 16), (16, 26), (26, 32))
 STEPS = [(a, b, c) for c in (0, 1) for a, b in FAR] + [(0, 0, 1)]
 
 
@@ -105,14 +107,148 @@
     return dot(chosen, rows_ref[...].astype(BF16), ((1,), (1,)))
 
 
+class PartSum:
+    def __init__(self, at, width, own, remote, along, above, layer, depth, partner, first, second, core, refs):
+        self.at, self.width, self.own, self.remote, self.along, self.above = at, width, own, remote, along, above
+        self.layer, self.depth, self.partner, self.first, self.second, self.core = (
+            layer, depth, partner, first, second, core
+        )
+        (
+            self.send1, self.recv1, self.send2, self.recv2, self.total, self.send3, self.recv3,
+            self.mine, self.recv4, self.whole, self.swap, self.both,
+            self.s1, self.r1, self.s2, self.r2, self.s3, self.r3, self.s4, self.r4, self.s5, self.r5,
+        ) = refs
+
+    def block(self, k, m):
+        a, b = lax.rem(self.first + k, 4), lax.rem(self.second + m, 4)
+        place = (1 - self.core) * (a * 4 + b) + self.core * (b * 4 + a)
+        return self.own[pl.ds(pl.multiple_of(place * TALL, 16), TALL), self.at : self.at + self.width]
+
+    def out1(self, i, k):
+        return self.remote(
+            self.send1.at[k - 1, i], self.recv1.at[k - 1, i], self.s1.at[k - 1, i], self.r1.at[k - 1, i],
+            self.along(k, 0),
+        )
+
+    def out2(self, m):
+        return self.remote(
+            self.send2.at[m - 1], self.recv2.at[m - 1], self.s2.at[m - 1], self.r2.at[m - 1], self.along(0, m)
+        )
+
+    def out3(self, k):
+        to = lax.rem(self.layer + k, self.depth)
+        return self.remote(
+            self.send3.at[to], self.recv3.at[k - 1], self.s3.at[k - 1], self.r3.at[k - 1], self.above(k)
+        )
+
+    def out4(self, k):
+        return self.remote(self.mine, self.recv4.at[k - 1], self.s4.at[k - 1], self.r4.at[k - 1], self.above(k))
+
+    def out5(self):
+        return self.remote(self.whole, self.swap, self.s5, self.r5, self.partner)
+
+    def turns(self):
+        return sorted(range(1, self.depth), key=lambda k: (-min(k, self.depth - k), k))
+
+    def begin(self):
+        def step(i, _):
+            for k in (1, 3, 2):
+                self.send1[k - 1, i] = self.block(k, i + 1).astype(BF16)
+                self.out1(i, k).start()
+            return 0
+
+        lax.fori_loop(0, 4, step, 0)
+
+    def gathered(self, i):
+        got = self.block(0, i + 1)
+        for k in (1, 2, 3):
+            self.out1(i, k).wait_recv()
+            got += self.recv1[k - 1, i].astype(F32)
+        return got
+
+    def second_axis(self):
+        for m in (1, 3, 2):
+            self.send2[m - 1] = self.gathered(m - 1).astype(BF16)
+            self.out2(m).start()
+        self.total[0:TALL, :] = self.gathered(3)
+        self.total[TALL:, :] = jnp.zeros((self.total.shape[0] - TALL, self.width), F32)
+
+    def over_layers(self):
+        kept = self.total[0:TALL, :]
+        for m in (1, 2, 3):
+            self.out2(m).wait_recv()
+            kept += self.recv2[m - 1].astype(F32)
+        self.total[0:TALL, :] = kept
+        self.send3[...] = self.total[...].astype(BF16).reshape(self.send3.shape)
+        for k in self.turns():
+            self.out3(k).start()
+
+    def share(self):
+        part = self.total[pl.ds(pl.multiple_of(self.layer * 16, 16), 16), :]
+        for k in range(1, self.depth):
+            self.out3(k).wait_recv()
+            part += self.recv3[k - 1].astype(F32)
+        self.mine[...] = part.astype(BF16)
+        for k in self.turns():
+            self.out4(k).start()
+        self.whole[self.layer] = self.mine[...]
+
+    def trade(self):
+        for k in range(1, self.depth):
+            self.out4(k).wait_recv()
+            self.whole[lax.rem(self.layer - k + self.depth, self.depth)] = self.recv4[k - 1]
+        self.out5().start()
+
+    def finish(self, out_ref):
+        row = pl.ds(pl.multiple_of(self.core * 56, 8), 56)
+        for ref, kind in ((self.whole, self.core), (self.swap, 1 - self.core)):
+            if ref is self.swap:
+                self.out5().wait_recv()
+            self.both[...] = ref[...].astype(F32).reshape(self.both.shape)
+            out_ref[:, pl.ds(pl.multiple_of(kind * HALF + self.at, 128), self.width)] = self.both[row, :]
+
+    def sent(self):
+        for k in (1, 2, 3):
+            for i in range(4):
+                self.out1(i, k).wait_send()
+            self.out2(k).wait_send()
+        for k in range(1, self.depth):
+            self.out3(k).wait_send()
+            self.out4(k).wait_send()
+        self.out5().wait_send()
+
+
+def part_scratch(width, depth):
+    block, thin = (TALL, width), (16, width)
+    dma = pltpu.SemaphoreType.DMA
+    return [
+        pltpu.VMEM((3, 4, *block), BF16),
+        pltpu.VMEM((3, 4, *block), BF16),
+        pltpu.VMEM((3, *block), BF16),
+        pltpu.VMEM((3, *block), BF16),
+        pltpu.VMEM((depth * 16, width), F32),
+        pltpu.VMEM((depth, *thin), BF16),
+        pltpu.VMEM((depth - 1, *thin), BF16),
+        pltpu.VMEM(thin, BF16),
+        pltpu.VMEM((depth - 1, *thin), BF16),
+        pltpu.VMEM((depth, *thin), BF16),
+        pltpu.VMEM((depth, *thin), BF16),
+        pltpu.VMEM((depth * 16, width), F32),
+        dma((3, 4)), dma((3, 4)),
+        dma((3,)), dma((3,)),
+        dma((depth - 1,)), dma((depth - 1,)),
+        dma((depth - 1,)), dma((depth - 1,)),
+        dma, dma,
+    ]
+
+
 def layer_kernel(
     holders, depth,
     count_ref, table_ref, src_ref, tgt_ref, rot_ref, len_ref, turns_ref, grads_ref, feats_ref, radial_ref, w_hbm,
     node_ref, out_ref,
     turn_ref, rows_ref, packed_ref, meta_out, meta_in, grad_out, grad_in, w_ref,
-    grad_ref, in_ref, pick_ref, scale_ref, acc_ref, own_ref, other_ref,
-    pair_ref, send1, recv1, part1, send2, recv2, total, send3, recv3, mine, recv4, whole, swap, both,
-    ws, ms, mr, gs, gr, ps, pr, s1, r1, s2, r2, s3, r3, s4, r4, s5, r5,
+    grad_ref, in_ref, pick_ref, scale_ref, acc_ref, own_ref, in_peer, grad_peer, half_in,
+    ws, ms, mr, gs, gr, is_, ir, hs, hr, *sums,
 ):
     me, layer = lax.axis_index("graph"), lax.axis_index("dp")
     core, place = lax.rem(me, 2), me // 2
@@ -195,63 +331,50 @@
     pack_nodes(feats_ref, packed_ref)
     for degree in range(DEG):
         part = jnp.where(in_degree(position, degree), packed_ref[...], 0.0).astype(BF16)
-        in_ref[:, degree * CH : (degree + 1) * CH] = (dot(pick, part) * scale_ref[...]).astype(BF16)
+        edge_in = dot(pick, part) * scale_ref[...]
+        in_ref[degree * CH : (degree + 1) * CH, :] = edge_in.T.astype(BF16)
     acc_ref[...] = jnp.zeros(acc_ref.shape, F32)
-    for k in range(1, holders):
-        grad_copy(k).wait_recv()
-    for degree in range(DEG):
-        cols = slice(degree * CH, (degree + 1) * CH)
-        grad_ref[:, cols] = grad_in[:, :, cols].astype(F32).reshape(rows, CH).astype(BF16)
 
     def columns(kind):
         return pl.ds(pl.multiple_of(kind * HALF, 128), HALF)
 
-    def weights_other(degree, _):
-        at = pl.ds(pl.multiple_of(degree * CH, CH), CH)
-        other_ref[at, :] = dot(in_ref[:, at], grad_ref[:, columns(1 - core)], ((0,), (0,))).astype(BF16)
-        return 0
-
-    lax.fori_loop(0, DEG, weights_other, 0)
-
-    def block_of(kind, n):
-        m, k = lax.rem(n // 4 + 1, 4), lax.rem(n + 1, 4)
-        a = lax.rem((1 - kind) * x + kind * y + k, 4)
-        b = lax.rem((1 - kind) * y + kind * x + m, 4)
-        return pl.ds(pl.multiple_of(chip(kind, a, b) * TALL, 16), TALL)
-
-    def pair(n):
-        return remote(other_ref.at[block_of(1 - core, n)], pair_ref.at[n], ps.at[n], pr.at[n], partner)
-
-    def pair_start(n, _):
-        pair(n).start()
-        return 0
-
-    lax.fori_loop(0, 16, pair_start, 0)
-
-    def weights_own(degree, _):
-        at = pl.ds(pl.multiple_of(degree * CH, CH), CH)
-        own_ref[at, :] = dot(in_ref[:, at], grad_ref[:, columns(core)], ((0,), (0,)))
-        return 0
-
-    lax.fori_loop(0, DEG, weights_own, 0)
-
-    def paired(n):
-        pair(n).wait_recv()
-        return own_ref[block_of(core, n), :] + pair_ref[n].astype(F32)
-
-    def out1(i, k):
-        return remote(send1.at[i, k - 1], recv1.at[i, k - 1], s1.at[i, k - 1], r1.at[i, k - 1], along(k, 0))
-
-    def step1(i, _):
-        for k in (1, 2, 3):
-            send1[i, k - 1] = paired(i * 4 + k - 1).astype(BF16)
-            out1(i, k).start()
-        part1[i] = paired(i * 4 + 3)
-        return 0
-
-    lax.fori_loop(0, 4, step1, 0)
-
-    load_w.wait()
+    in_copy = remote(in_ref, in_peer, is_, ir, partner)
+    in_copy.start()
+
+    def half_copy(n):
+        slabs = pl.ds(GROUPS[n][0], GROUPS[n][1] - GROUPS[n][0])
+        return remote(
+            grad_in.at[slabs, :, columns(1 - core)], half_in.at[slabs], hs.at[n], hr.at[n], partner
+        )
+
+    def arrive(n):
+        begin, end = GROUPS[n]
+        for k in range(max(begin, 1), end):
+            grad_copy(k).wait_recv()
+        half_copy(n).start()
+        for degree in range(DEG):
+            cols = slice(degree * CH, (degree + 1) * CH)
+            slab = grad_in[begin:end, :, cols].astype(F32)
+            grad_ref[begin * CAP : end * CAP, cols] = slab.reshape(-1, CH).astype(BF16)
+
+    def arrive_peer(n):
+        begin, end = GROUPS[n]
+        half_copy(n).wait_recv()
+        for at, width in PARTS:
+            slab = half_in[begin:end, :, at : at + width].astype(F32)
+            grad_peer[begin * CAP : end * CAP, at : at + width] = slab.reshape(-1, width).astype(BF16)
+
+    def weights(p):
+        cols = pl.ds(pl.multiple_of(core * HALF + p.at, 128), p.width)
+
+        def terms(t, _):
+            tall = pl.ds(pl.multiple_of(t * (WIDTH // 2), 128), WIDTH // 2)
+            term = dot(in_ref[tall, :], grad_ref[:, cols])
+            term += dot(in_peer[tall, :], grad_peer[:, p.at : p.at + p.width])
+            own_ref[tall, p.at : p.at + p.width] = term
+            return 0
+
+        lax.fori_loop(0, 2, terms, 0)
 
     def backward(degree, _):
         at = pl.ds(pl.multiple_of(degree * CH, CH), CH)
@@ -261,79 +384,42 @@
         acc_ref[...] += jnp.where(in_degree(position, degree), term, 0.0)
         return 0
 
-    lax.fori_loop(0, DEG, backward, 0)
+    for n in range(len(GROUPS)):
+        arrive(n)
+    in_copy.wait_recv()
+    for n in range(len(GROUPS)):
+        arrive_peer(n)
+    each = len(sums) // len(PARTS)
+    parts = [
+        PartSum(at, width, own_ref, remote, along, above, layer, depth, partner, first, second, core,
+                sums[n * each : (n + 1) * each])
+        for n, (at, width) in enumerate(PARTS)
+    ]
+    for p in parts:
+        weights(p)
+        p.begin()
+    load_w.wait()
+    lax.fori_loop(0, 4, backward, 0)
+    parts[0].second_axis()
+    lax.fori_loop(4, DEG, backward, 0)
     for q in range(ROWS):
         node_ref[q] = acc_ref[q * 64 : q * 64 + COEF, :]
-
-    def gathered(i):
-        got = part1[i]
-        for k in (1, 2, 3):
-            out1(i, k).wait_recv()
-            got += recv1[i, k - 1].astype(F32)
-        return got
-
-    def out2(m):
-        return remote(send2.at[m - 1], recv2.at[m - 1], s2.at[m - 1], r2.at[m - 1], along(0, m))
-
-    for m in (1, 2, 3):
-        send2[m - 1] = gathered(m - 1).astype(BF16)
-        out2(m).start()
-    kept = gathered(3)
-    for m in (1, 2, 3):
-        out2(m).wait_recv()
-        kept += recv2[m - 1].astype(F32)
-    total[0:TALL, :] = kept
-    total[TALL:, :] = jnp.zeros((total.shape[0] - TALL, HALF), F32)
-    send3[...] = total[...].astype(BF16).reshape(send3.shape)
-
-    def out3(k):
-        return remote(
-            send3.at[lax.rem(layer + k, depth)], recv3.at[k - 1], s3.at[k - 1], r3.at[k - 1], above(k)
-        )
-
-    for k in range(1, depth):
-        out3(k).start()
-    part = total[pl.ds(pl.multiple_of(layer * 16, 16), 16), :]
-    for k in range(1, depth):
-        out3(k).wait_recv()
-        part += recv3[k - 1].astype(F32)
-    mine[...] = part.astype(BF16)
-
-    def out4(k):
-        return remote(mine, recv4.at[k - 1], s4.at[k - 1], r4.at[k - 1], above(k))
-
-    for k in range(1, depth):
-        out4(k).start()
-    whole[layer] = mine[...]
-    for k in range(1, depth):
-        out4(k).wait_recv()
-        whole[lax.rem(layer - k + depth, depth)] = recv4[k - 1]
-    out5 = remote(whole, swap, s5, r5, partner)
-    out5.start()
-    row = pl.ds(pl.multiple_of(core * 56, 8), 56)
-    both[...] = whole[...].astype(F32).reshape(both.shape)
-    out_ref[:, columns(core)] = both[row, :]
-    out5.wait_recv()
-    both[...] = swap[...].astype(F32).reshape(both.shape)
-    out_ref[:, columns(1 - core)] = both[row, :]
+    stages = ("second_axis", "over_layers", "share", "trade")
+    for wave in range(1, len(stages) + len(parts) - 1):
+        for n, p in enumerate(parts):
+            if 0 <= wave - n < len(stages):
+                getattr(p, stages[wave - n])()
+    for p in parts:
+        p.finish(out_ref)
 
     for k in range(1, holders):
         meta_copy(k).wait_send()
         grad_copy(k).wait_send()
-
-    def pair_done(n, _):
-        pair(n).wait_send()
-        return 0
-
-    lax.fori_loop(0, 16, pair_done, 0)
-    for k in (1, 2, 3):
-        for i in range(4):
-            out1(i, k).wait_send()
-        out2(k).wait_send()
-    for k in range(1, depth):
-        out3(k).wait_send()
-        out4(k).wait_send()
-    out5.wait_send()
+    in_copy.wait_send()
+    for n in range(len(GROUPS)):
+        half_copy(n).wait_send()
+    for p in parts:
+        p.sent()
 
 
 def per_device(
@@ -343,7 +429,6 @@
     slots = edge_src.shape[1]
     turns = rotations.transpose(1, 2, 0)
     rows = holders * CAP
-    block = (TALL, HALF)
     vmem = pl.BlockSpec(memory_space=pltpu.VMEM)
     dma = pltpu.SemaphoreType.DMA
     buffer = pltpu.VMEM
@@ -365,35 +450,20 @@
             buffer((holders, CAP, WIDTH), BF16),
             buffer((WIDTH, WIDTH), BF16),
             buffer((rows, WIDTH), BF16),
-            buffer((rows, WIDTH), BF16),
+            buffer((WIDTH, rows), BF16),
             buffer((SPAN, rows), BF16),
             buffer((rows, CH), F32),
             buffer((SPAN, CH), F32),
             buffer((WIDTH, HALF), F32),
-            buffer((WIDTH, HALF), BF16),
-            buffer((16, *block), BF16),
-            buffer((4, 3, *block), BF16),
-            buffer((4, 3, *block), BF16),
-            buffer((4, *block), F32),
-            buffer((3, *block), BF16),
-            buffer((3, *block), BF16),
-            buffer((depth * 16, HALF), F32),
-            buffer((depth, 16, HALF), BF16),
-            buffer((depth - 1, 16, HALF), BF16),
-            buffer((16, HALF), BF16),
-            buffer((depth - 1, 16, HALF), BF16),
-            buffer((depth, 16, HALF), BF16),
-            buffer((depth, 16, HALF), BF16),
-            buffer((depth * 16, HALF), F32),
+            buffer((WIDTH, rows), BF16),
+            buffer((rows, HALF), BF16),
+            buffer((holders, CAP, HALF), BF16),
             dma,
             dma((holders,)), dma((holders,)),
             dma((holders,)), dma((holders,)),
-            dma((16,)), dma((16,)),
-            dma((4, 3)), dma((4, 3)),
-            dma((3,)), dma((3,)),
-            dma((depth - 1,)), dma((depth - 1,)),
-            dma((depth - 1,)), dma((depth - 1,)),
             dma, dma,
+            dma((len(GROUPS),)), dma((len(GROUPS),)),
+            *(shape for _, width in PARTS for shape in part_scratch(width, depth)),
         ],
         compiler_params=pltpu.CompilerParams(
             collective_id=0, has_side_effects=True, vmem_limit_bytes=VMEM_LIMIT

time: 106 us -> 99 us (0.934)
  Pallas kernels: 101 us -> 93.7 us
    pallas_call x1, Pallas kernels: 101 us -> 93.7 us  [per_device(): pl.pallas_call(functools.partial(layer_kernel, holders, depth), out_shape...]
where the time goes in v3:
time: 99 us; the launch traced here: 98.8 us
  Pallas kernels  93.7 us (95%)
  local copies, waits for them, and re-layouts  3.86 us (4%)
  between operations  1.29 us (1%)
    pallas_call x1, Pallas kernels, per_device(): pl.pallas_call(functools.partial(layer_kernel, holders, depth), out_shape...  93.7 us
    unnamed x2, local copies, waits for them, and re-layouts  3.86 us

profile of v3, /device:TPU:1, one launch (start us, length us, event | category | flops | bytes accessed | tf_op | source)
XLA Modules:
  0.0 98.8 jit_solution(2323493378109228239)
XLA Ops:
  1.3 93.7 %layer.1 = (f32[7,49,256]{2,1,0:T(8,128)}, f32[56,1792]{1,0:T(8,128)}) custom-call(s32[1,1]{1,0:T(1,128)S(6)} %copy.15.count_ref, s32[1,224]{1,0:T(1,128)} %table_ref.1, s32[1,512]{1,0:T(1,128)} %src_ref.1, s32[1,512]{1,0:T(1,128)} %tgt_ref.1, s32[1,512]{1,0:T(1,128)} %rot_ref.1, f32[1,512]{1,0:T(1,128)} %len_ref.1, bf16[7,49,2048]{2,1,0:T(8,128)(2,1)} %bitcast.4, ...), custom_call_target="tpu_custom_call" | custom-call | tf_op jit(solution)/shard_map/layer/pallas_call | solution.py:435
  95.0 2.1 %copy.13 = f32[1,7,49,256]{3,0,2,1:T(1,128)} copy(f32[1,7,49,256]{3,2,1,0:T(8,128)} %bitcast.5) | data formatting | bytes 702464
  97.1 1.8 %copy.16 = f32[56,1792]{1,0:T(8,128)} copy(f32[56,1792]{1,0:T(8,128)} %get-tuple-element.11) | data formatting | bytes 802816

commit v4 on v3

--- a/solution.py
+++ b/solution.py
@@ -17,7 +17,7 @@
 META = 128
 HALF = WIDTH // 2
 TALL = 112
-PARTS = ((0, 512), (512, 384))
+PARTS = ((0, 384), (384, 512))
 SPAN = 64 * ROWS
 F32, BF16, I32 = jnp.float32, jnp.bfloat16, jnp.int32
 MESH = pl.DeviceIdType.MESH
@@ -108,15 +108,16 @@
 
 
 class PartSum:
-    def __init__(self, at, width, own, remote, along, above, layer, depth, partner, first, second, core, refs):
+    def __init__(self, at, width, own, remote, along, above, layer, depth, partner, site, first, second, core, refs):
         self.at, self.width, self.own, self.remote, self.along, self.above = at, width, own, remote, along, above
+        self.site = site
         self.layer, self.depth, self.partner, self.first, self.second, self.core = (
             layer, depth, partner, first, second, core
         )
         (
             self.send1, self.recv1, self.send2, self.recv2, self.total, self.send3, self.recv3,
-            self.mine, self.recv4, self.whole, self.swap, self.both,
-            self.s1, self.r1, self.s2, self.r2, self.s3, self.r3, self.s4, self.r4, self.s5, self.r5,
+            self.mine, self.recv4, self.held,
+            self.s1, self.r1, self.s2, self.r2, self.s3, self.r3, self.s4, self.r4,
         ) = refs
 
     def block(self, k, m):
@@ -125,9 +126,10 @@
         return self.own[pl.ds(pl.multiple_of(place * TALL, 16), TALL), self.at : self.at + self.width]
 
     def out1(self, i, k):
+        to = k if k != 2 else 1 if i < 2 else 3
         return self.remote(
             self.send1.at[k - 1, i], self.recv1.at[k - 1, i], self.s1.at[k - 1, i], self.r1.at[k - 1, i],
-            self.along(k, 0),
+            self.along(to, 0),
         )
 
     def out2(self, m):
@@ -142,26 +144,33 @@
         )
 
     def out4(self, k):
-        return self.remote(self.mine, self.recv4.at[k - 1], self.s4.at[k - 1], self.r4.at[k - 1], self.above(k))
-
-    def out5(self):
-        return self.remote(self.whole, self.swap, self.s5, self.r5, self.partner)
+        half = self.depth // 2
+        slot = lax.rem(self.layer, half)
+        return self.remote(
+            self.mine, self.recv4.at[self.core, slot], self.s4.at[k], self.r4.at[self.core, slot],
+            {"graph": self.site + self.layer // half, "dp": lax.rem(self.layer + k, self.depth)},
+        )
+
+    def is_holder(self):
+        return self.layer // (self.depth // 2) == self.core
 
     def turns(self):
         return sorted(range(1, self.depth), key=lambda k: (-min(k, self.depth - k), k))
 
     def begin(self):
-        def step(i, _):
-            for k in (1, 3, 2):
-                self.send1[k - 1, i] = self.block(k, i + 1).astype(BF16)
-                self.out1(i, k).start()
-            return 0
-
-        lax.fori_loop(0, 4, step, 0)
+        for k, i in ((2, 0), (2, 2), (2, 1), (2, 3), (1, 2), (3, 0), (1, 3), (3, 1)):
+            self.send1[k - 1, i] = self.block(k, i + 1).astype(BF16)
+            self.out1(i, k).start()
+
+    def merge(self):
+        for k, i in ((1, 0), (3, 2), (1, 1), (3, 3)):
+            self.out1(i, 2).wait_recv()
+            self.send1[k - 1, i] = (self.block(k, i + 1) + self.recv1[1, i].astype(F32)).astype(BF16)
+            self.out1(i, k).start()
 
     def gathered(self, i):
         got = self.block(0, i + 1)
-        for k in (1, 2, 3):
+        for k in (1, 3):
             self.out1(i, k).wait_recv()
             got += self.recv1[k - 1, i].astype(F32)
         return got
@@ -170,15 +179,17 @@
         for m in (1, 3, 2):
             self.send2[m - 1] = self.gathered(m - 1).astype(BF16)
             self.out2(m).start()
-        self.total[0:TALL, :] = self.gathered(3)
-        self.total[TALL:, :] = jnp.zeros((self.total.shape[0] - TALL, self.width), F32)
+        self.held[...] = self.gathered(3)
 
     def over_layers(self):
-        kept = self.total[0:TALL, :]
+        kept = self.held[...]
         for m in (1, 2, 3):
             self.out2(m).wait_recv()
             kept += self.recv2[m - 1].astype(F32)
-        self.total[0:TALL, :] = kept
+        half, mid = TALL // 2, self.total.shape[0] // 2
+        self.total[...] = jnp.zeros(self.total.shape, F32)
+        self.total[0:half, :] = kept[0:half]
+        self.total[mid : mid + half, :] = kept[half:]
         self.send3[...] = self.total[...].astype(BF16).reshape(self.send3.shape)
         for k in self.turns():
             self.out3(k).start()
@@ -191,21 +202,31 @@
         self.mine[...] = part.astype(BF16)
         for k in self.turns():
             self.out4(k).start()
-        self.whole[self.layer] = self.mine[...]
-
-    def trade(self):
-        for k in range(1, self.depth):
-            self.out4(k).wait_recv()
-            self.whole[lax.rem(self.layer - k + self.depth, self.depth)] = self.recv4[k - 1]
-        self.out5().start()
+
+        @pl.when(jnp.logical_not(self.is_holder()))
+        def _():
+            self.out4(0).start()
+
+        @pl.when(self.is_holder())
+        def _():
+            self.recv4[self.core, lax.rem(self.layer, self.depth // 2)] = self.mine[...]
 
     def finish(self, out_ref):
-        row = pl.ds(pl.multiple_of(self.core * 56, 8), 56)
-        for ref, kind in ((self.whole, self.core), (self.swap, 1 - self.core)):
-            if ref is self.swap:
-                self.out5().wait_recv()
-            self.both[...] = ref[...].astype(F32).reshape(self.both.shape)
-            out_ref[:, pl.ds(pl.multiple_of(kind * HALF + self.at, 128), self.width)] = self.both[row, :]
+        half = self.depth // 2
+        for kind in (0, 1):
+            for slot in range(half):
+                here = (self.core * half + slot == self.layer) & (self.core == kind)
+
+                @pl.when(jnp.logical_not(here))
+                def _(kind=kind, slot=slot):
+                    self.remote(
+                        self.mine, self.recv4.at[kind, slot], self.s4.at[0], self.r4.at[kind, slot], self.partner
+                    ).wait_recv()
+
+                tall = min(16, out_ref.shape[0] - slot * 16)
+                at = kind * HALF + self.at
+                rows = self.recv4[kind, slot].astype(F32)
+                out_ref[slot * 16 : slot * 16 + tall, at : at + self.width] = rows[0:tall]
 
     def sent(self):
         for k in (1, 2, 3):
@@ -215,7 +236,10 @@
         for k in range(1, self.depth):
             self.out3(k).wait_send()
             self.out4(k).wait_send()
-        self.out5().wait_send()
+
+        @pl.when(jnp.logical_not(self.is_holder()))
+        def _():
+            self.out4(0).wait_send()
 
 
 def part_scratch(width, depth):
@@ -230,15 +254,12 @@
         pltpu.VMEM((depth, *thin), BF16),
         pltpu.VMEM((depth - 1, *thin), BF16),
         pltpu.VMEM(thin, BF16),
-        pltpu.VMEM((depth - 1, *thin), BF16),
-        pltpu.VMEM((depth, *thin), BF16),
-        pltpu.VMEM((depth, *thin), BF16),
-        pltpu.VMEM((depth * 16, width), F32),
+        pltpu.VMEM((2, depth // 2, *thin), BF16),
+        pltpu.VMEM(block, F32),
         dma((3, 4)), dma((3, 4)),
         dma((3,)), dma((3,)),
         dma((depth - 1,)), dma((depth - 1,)),
-        dma((depth - 1,)), dma((depth - 1,)),
-        dma, dma,
+        dma((depth,)), dma((2, depth // 2)),
     ]
 
 
@@ -283,12 +304,13 @@
         pl.semaphore_signal(barrier, inc=1, device_id={"graph": index(a, b, c)}, device_id_type=MESH)
     for k in range(1, depth):
         pl.semaphore_signal(barrier, inc=1, device_id=above(k), device_id_type=MESH)
+        pl.semaphore_signal(barrier, inc=1, device_id={**partner, **above(k)}, device_id_type=MESH)
 
     meta = find_meta(
         holders, count_ref, table_ref, src_ref, tgt_ref, rot_ref, len_ref, turns_ref, turn_ref, rows_ref
     )
     meta_out[...] = meta.reshape(holders, CAP, META).astype(BF16)
-    pl.semaphore_wait(barrier, len(STEPS) + depth - 1)
+    pl.semaphore_wait(barrier, len(STEPS) + 2 * (depth - 1))
 
     def meta_copy(k):
         peer = index(*STEPS[k - 1])
@@ -391,24 +413,27 @@
         arrive_peer(n)
     each = len(sums) // len(PARTS)
     parts = [
-        PartSum(at, width, own_ref, remote, along, above, layer, depth, partner, first, second, core,
+        PartSum(at, width, own_ref, remote, along, above, layer, depth, partner, place * 2, first, second, core,
                 sums[n * each : (n + 1) * each])
         for n, (at, width) in enumerate(PARTS)
     ]
     for p in parts:
         weights(p)
         p.begin()
+    parts[0].merge()
     load_w.wait()
-    lax.fori_loop(0, 4, backward, 0)
+    lax.fori_loop(0, 3, backward, 0)
+    parts[1].merge()
+    lax.fori_loop(3, 5, backward, 0)
     parts[0].second_axis()
-    lax.fori_loop(4, DEG, backward, 0)
+    lax.fori_loop(5, DEG, backward, 0)
     for q in range(ROWS):
         node_ref[q] = acc_ref[q * 64 : q * 64 + COEF, :]
-    stages = ("second_axis", "over_layers", "share", "trade")
-    for wave in range(1, len(stages) + len(parts) - 1):
-        for n, p in enumerate(parts):
-            if 0 <= wave - n < len(stages):
-                getattr(p, stages[wave - n])()
+    parts[0].over_layers()
+    parts[1].second_axis()
+    parts[0].share()
+    parts[1].over_layers()
+    parts[1].share()
     for p in parts:
         p.finish(out_ref)
 

time: 99 us -> 96.4 us (0.974)
  Pallas kernels: 93.7 us -> 91 us
    pallas_call x1, Pallas kernels: 93.7 us -> 91 us  [per_device(): pl.pallas_call(functools.partial(layer_kernel, holders, depth), out_shape...]
where the time goes in v4:
time: 96.4 us; the launch traced here: 96.2 us
  Pallas kernels  91 us (94%)
  local copies, waits for them, and re-layouts  3.86 us (4%)
  between operations  1.29 us (1%)
    pallas_call x1, Pallas kernels, per_device(): pl.pallas_call(functools.partial(layer_kernel, holders, depth), out_shape...  91 us
    unnamed x2, local copies, waits for them, and re-layouts  3.86 us

profile of v4, /device:TPU:1, one launch (start us, length us, event | category | flops | bytes accessed | tf_op | source)
XLA Modules:
  0.0 96.2 jit_solution(1781166865094482978)
XLA Ops:
  1.3 91.0 %layer.1 = (f32[7,49,256]{2,1,0:T(8,128)}, f32[56,1792]{1,0:T(8,128)}) custom-call(s32[1,1]{1,0:T(1,128)S(6)} %copy.15.count_ref, s32[1,224]{1,0:T(1,128)} %table_ref.1, s32[1,512]{1,0:T(1,128)} %src_ref.1, s32[1,512]{1,0:T(1,128)} %tgt_ref.1, s32[1,512]{1,0:T(1,128)} %rot_ref.1, f32[1,512]{1,0:T(1,128)} %len_ref.1, bf16[7,49,2048]{2,1,0:T(8,128)(2,1)} %bitcast.4, ...), custom_call_target="tpu_custom_call" | custom-call | tf_op jit(solution)/shard_map/layer/pallas_call | solution.py:460
  92.3 2.1 %copy.13 = f32[1,7,49,256]{3,0,2,1:T(1,128)} copy(f32[1,7,49,256]{3,2,1,0:T(8,128)} %bitcast.5) | data formatting | bytes 702464
  94.4 1.8 %copy.16 = f32[56,1792]{1,0:T(8,128)} copy(f32[56,1792]{1,0:T(8,128)} %get-tuple-element.11) | data formatting | bytes 802816

commit v5 on v4

--- a/solution.py
+++ b/solution.py
@@ -228,13 +228,18 @@
                 rows = self.recv4[kind, slot].astype(F32)
                 out_ref[slot * 16 : slot * 16 + tall, at : at + self.width] = rows[0:tall]
 
-    def sent(self):
+    def sent_chips(self):
         for k in (1, 2, 3):
             for i in range(4):
                 self.out1(i, k).wait_send()
             self.out2(k).wait_send()
+
+    def sent_layers(self):
         for k in range(1, self.depth):
             self.out3(k).wait_send()
+
+    def sent_holders(self):
+        for k in range(1, self.depth):
             self.out4(k).wait_send()
 
         @pl.when(jnp.logical_not(self.is_holder()))
@@ -430,21 +435,24 @@
     for q in range(ROWS):
         node_ref[q] = acc_ref[q * 64 : q * 64 + COEF, :]
     parts[0].over_layers()
-    parts[1].second_axis()
-    parts[0].share()
-    parts[1].over_layers()
-    parts[1].share()
-    for p in parts:
-        p.finish(out_ref)
-
     for k in range(1, holders):
         meta_copy(k).wait_send()
         grad_copy(k).wait_send()
     in_copy.wait_send()
     for n in range(len(GROUPS)):
         half_copy(n).wait_send()
-    for p in parts:
-        p.sent()
+    parts[1].second_axis()
+    parts[0].share()
+    parts[0].sent_chips()
+    parts[1].over_layers()
+    parts[0].sent_layers()
+    parts[1].sent_chips()
+    parts[0].finish(out_ref)
+    parts[1].share()
+    parts[0].sent_holders()
+    parts[1].sent_layers()
+    parts[1].finish(out_ref)
+    parts[1].sent_holders()
 
 
 def per_device(

time: 96.4 us -> 95.7 us (level)
  no operation moved by 1% of the time
where the time goes in v5:
time: 95.7 us; the launch traced here: 95.5 us
  Pallas kernels  90.3 us (94%)
  local copies, waits for them, and re-layouts  3.86 us (4%)
  between operations  1.29 us (1%)
    pallas_call x1, Pallas kernels, per_device(): pl.pallas_call(functools.partial(layer_kernel, holders, depth), out_shape...  90.3 us
    unnamed x2, local copies, waits for them, and re-layouts  3.86 us

profile of v5, /device:TPU:1, one launch (start us, length us, event | category | flops | bytes accessed | tf_op | source)
XLA Modules:
  0.0 95.5 jit_solution(44299485062577946)
XLA Ops:
  1.3 90.3 %layer.1 = (f32[7,49,256]{2,1,0:T(8,128)}, f32[56,1792]{1,0:T(8,128)}) custom-call(s32[1,1]{1,0:T(1,128)S(6)} %copy.15.count_ref, s32[1,224]{1,0:T(1,128)} %table_ref.1, s32[1,512]{1,0:T(1,128)} %src_ref.1, s32[1,512]{1,0:T(1,128)} %tgt_ref.1, s32[1,512]{1,0:T(1,128)} %rot_ref.1, f32[1,512]{1,0:T(1,128)} %len_ref.1, bf16[7,49,2048]{2,1,0:T(8,128)(2,1)} %bitcast.4, ...), custom_call_target="tpu_custom_call" | custom-call | tf_op jit(solution)/shard_map/layer/pallas_call | solution.py:468
  91.6 2.1 %copy.13 = f32[1,7,49,256]{3,0,2,1:T(1,128)} copy(f32[1,7,49,256]{3,2,1,0:T(8,128)} %bitcast.5) | data formatting | bytes 702464
  93.7 1.8 %copy.16 = f32[56,1792]{1,0:T(8,128)} copy(f32[56,1792]{1,0:T(8,128)} %get-tuple-element.11) | data formatting | bytes 802816

commit v6 on v5

--- a/solution.py
+++ b/solution.py
@@ -82,10 +82,10 @@
     place = jnp.where(live, holder * CAP + rank.astype(I32), -1)
     chosen = onehot(iota((holders * CAP, slots), 0) == place)
 
-    total = turns_ref[0].astype(F32)
+    total = turns_ref[0]
     for degree in range(1, DEG):
-        total += turns_ref[degree].astype(F32)
-    turn_ref[...] = total.astype(BF16)
+        total += turns_ref[degree]
+    turn_ref[...] = total
     step = 512
     turned = jnp.zeros((COEF, slots), F32)
     for start in range(0, turns_ref.shape[2], step):
@@ -391,14 +391,19 @@
             slab = half_in[begin:end, :, at : at + width].astype(F32)
             grad_peer[begin * CAP : end * CAP, at : at + width] = slab.reshape(-1, width).astype(BF16)
 
-    def weights(p):
+    def weights(p, own, peer):
         cols = pl.ds(pl.multiple_of(core * HALF + p.at, 128), p.width)
+        there = slice(p.at, p.at + p.width)
 
         def terms(t, _):
             tall = pl.ds(pl.multiple_of(t * (WIDTH // 2), 128), WIDTH // 2)
-            term = dot(in_ref[tall, :], grad_ref[:, cols])
-            term += dot(in_peer[tall, :], grad_peer[:, p.at : p.at + p.width])
-            own_ref[tall, p.at : p.at + p.width] = term
+            if own:
+                term = dot(in_ref[tall, :], grad_ref[:, cols])
+            else:
+                term = own_ref[tall, there]
+            if peer:
+                term += dot(in_peer[tall, :], grad_peer[:, there])
+            own_ref[tall, there] = term
             return 0
 
         lax.fori_loop(0, 2, terms, 0)
@@ -411,20 +416,24 @@
         acc_ref[...] += jnp.where(in_degree(position, degree), term, 0.0)
         return 0
 
-    for n in range(len(GROUPS)):
-        arrive(n)
-    in_copy.wait_recv()
-    for n in range(len(GROUPS)):
-        arrive_peer(n)
     each = len(sums) // len(PARTS)
     parts = [
         PartSum(at, width, own_ref, remote, along, above, layer, depth, partner, place * 2, first, second, core,
                 sums[n * each : (n + 1) * each])
         for n, (at, width) in enumerate(PARTS)
     ]
-    for p in parts:
-        weights(p)
-        p.begin()
+    arrive(0)
+    arrive(1)
+    arrive_peer(0)
+    arrive(2)
+    weights(parts[0], True, False)
+    in_copy.wait_recv()
+    arrive_peer(1)
+    arrive_peer(2)
+    weights(parts[0], False, True)
+    parts[0].begin()
+    weights(parts[1], True, True)
+    parts[1].begin()
     parts[0].merge()
     load_w.wait()
     lax.fori_loop(0, 3, backward, 0)

time: 95.7 us -> 94.7 us (0.990)
  Pallas kernels: 90.3 us -> 89.3 us
    pallas_call x1, Pallas kernels: 90.3 us -> 89.3 us  [per_device(): pl.pallas_call(functools.partial(layer_kernel, holders, depth), out_shape...]
where the time goes in v6:
time: 94.7 us; the launch traced here: 94.5 us
  Pallas kernels  89.3 us (94%)
  local copies, waits for them, and re-layouts  3.86 us (4%)
  between operations  1.29 us (1%)
    pallas_call x1, Pallas kernels, per_device(): pl.pallas_call(functools.partial(layer_kernel, holders, depth), out_shape...  89.3 us
    unnamed x2, local copies, waits for them, and re-layouts  3.86 us

profile of v6, /device:TPU:1, one launch (start us, length us, event | category | flops | bytes accessed | tf_op | source)
XLA Modules:
  0.0 94.5 jit_solution(15165835321088478003)
XLA Ops:
  1.3 89.3 %layer.1 = (f32[7,49,256]{2,1,0:T(8,128)}, f32[56,1792]{1,0:T(8,128)}) custom-call(s32[1,1]{1,0:T(1,128)S(6)} %copy.15.count_ref, s32[1,224]{1,0:T(1,128)} %table_ref.1, s32[1,512]{1,0:T(1,128)} %src_ref.1, s32[1,512]{1,0:T(1,128)} %tgt_ref.1, s32[1,512]{1,0:T(1,128)} %rot_ref.1, f32[1,512]{1,0:T(1,128)} %len_ref.1, bf16[7,49,2048]{2,1,0:T(8,128)(2,1)} %bitcast.4, ...), custom_call_target="tpu_custom_call" | custom-call | tf_op jit(solution)/shard_map/layer/pallas_call | solution.py:477
  90.6 2.1 %copy.13 = f32[1,7,49,256]{3,0,2,1:T(1,128)} copy(f32[1,7,49,256]{3,2,1,0:T(8,128)} %bitcast.5) | data formatting | bytes 702464
  92.7 1.8 %copy.16 = f32[56,1792]{1,0:T(8,128)} copy(f32[56,1792]{1,0:T(8,128)} %get-tuple-element.11) | data formatting | bytes 802816
